TPU v7x, 32 devices: a whole 2x2x4 slice. The times are simulated.
32 devices in a mesh: clips: 2 (over y), patch: 4 (over z), span: 2 (over x), chan: 2 (over core).
Axes of the slice: x: 2, y: 2, z: 4, core: 2. Of those that a mesh axis runs over, the one named last changes fastest.
Arguments:
- latent_tiles: bfloat16 [4, 256, 4, 384], P(('clips', 'span'), 'patch'), parts along dimension 0, may hold values from -12 to 12
- route: int32 [4, 256], P(('clips', 'span')), parts along dimension 0, may hold values from 0 to 255, as said below
- w_query: bfloat16 [384, 384], replicated, may hold values from -0.5 to 4.6
- w_keyval: bfloat16 [384, 768], replicated, may hold values from -0.5 to 4.6
- conv_weight: bfloat16 [3, 3, 3, 384, 384], P(None, None, None, None, 'chan'), may hold values from -0.0625 to 0.0625
Outputs:
- decoded: bfloat16 [8, 8, 64, 384], P(('clips', 'span'), 'patch', None, 'chan'), parts along dimension 0
There are 2 independent parts, one for each index of `clips`. A program takes and returns all parts, laid end to end along the dimension named above; an argument that names none is the same for every part. Nothing has to cross between parts.
Inputs may be any that keep to these rules, and one draw needn't show every extreme that they name: `route`: each span's row is a permutation of 0 .. 255. The 64 tiles of positions j * 64 to (j + 1) * 64 - 1 go to at most 32 per owner, and in every span some such group sends exactly 32 to one owner.
All inputs are finite; a program needn't handle non-finite values.
Results may differ from a plain program's by a relative error of at most 0.0065.
Values may be sent and summed in bfloat16 or wider, within the bound.
A program may use at most 64 MiB of HBM per device.

v0:
```python
import math

import jax
import jax.numpy as jnp
from jax import lax
from jax.sharding import PartitionSpec as P

C = 384
W = 64
RD = 2
FD = 2


epsilon = 1e-06


def shifted(x, axis, by):
    length = lax.axis_size(axis)
    pairs = [(i, i + by) for i in range(length) if 0 <= i + by < length]
    return lax.ppermute(x, axis, pairs)


def with_halo(cells, sides, width):
    for axis, dim in sides:
        count = lax.axis_size(axis)
        ends = count - 1
        head = lax.slice_in_dim(cells, 0, width, axis=dim)
        tail = lax.slice_in_dim(cells, cells.shape[dim] - width, cells.shape[dim], axis=dim)
        cells = jnp.concatenate(
            [
                lax.ppermute(tail, axis, [(i, (i + 1) % count) for i in range(ends)]),
                cells,
                lax.ppermute(head, axis, [((i + 1) % count, i) for i in range(ends)]),
            ],
            axis=dim,
        )
    return cells


def scaled_rms(values):
    wide = values.astype(jnp.float32)
    return wide / jnp.sqrt(jnp.mean(wide * wide, axis=-1, keepdims=True) + epsilon)


def fold_scores(carry, queries, key_rows, value_rows):
    run_max, run_total, run_acc = carry
    scale = 1.0 / math.sqrt(queries.shape[-1])
    scores = (
        jnp.einsum("fqc,fkc->fqk", queries, key_rows, preferred_element_type=jnp.float32) * scale
    )
    new_max = jnp.max(scores, axis=-1)
    factor = jnp.exp(run_max - new_max)
    powers = jnp.exp(scores - new_max[..., None])
    run_total = run_total * factor + jnp.sum(powers, axis=-1)
    weights = powers.astype(jnp.bfloat16)
    run_acc = run_acc * factor[..., None] + jnp.einsum(
        "fqk,fkc->fqc", weights, value_rows, preferred_element_type=jnp.float32
    )
    return (new_max, run_total, run_acc)


def local(latent_tiles, route, w_query, w_keyval, conv_weight):
    patch_count = lax.axis_size("patch")
    patch_index = lax.axis_index("patch")
    chan_count = lax.axis_size("chan")
    chan_index = lax.axis_index("chan")
    table = route[0]
    frames_core = FD // chan_count
    cell_count = RD * W
    start_carry = (
        jnp.full((frames_core, cell_count), -jnp.inf, jnp.float32),
        jnp.zeros((frames_core, cell_count), jnp.float32),
        jnp.zeros((frames_core, cell_count, C), jnp.float32),
    )
    every_tile = lax.all_gather(latent_tiles, "patch", axis=1, tiled=True)[0]
    tile_total = every_tile.shape[0]
    inverse = (
        jnp.zeros((tile_total,), jnp.int32).at[table].set(jnp.arange(tile_total, dtype=jnp.int32))
    )
    placed = jnp.take(every_tile, inverse, axis=0).reshape(patch_count, FD, RD, W, C)
    whole = placed.transpose(1, 0, 2, 3, 4).reshape(FD, patch_count * RD, W, C)
    features = lax.dynamic_slice_in_dim(whole, patch_index * RD, RD, 1)
    own_frames = lax.dynamic_slice_in_dim(features, chan_index * frames_core, frames_core, 0)
    frame_all = lax.dynamic_slice_in_dim(whole, chan_index * frames_core, frames_core, 0)
    normed_all = scaled_rms(frame_all).astype(jnp.bfloat16)
    normed = lax.dynamic_slice_in_dim(normed_all, patch_index * RD, RD, 1).reshape(
        frames_core, cell_count, C
    )
    queries = jnp.einsum("fnc,cd->fnd", normed, w_query, preferred_element_type=jnp.float32).astype(
        jnp.bfloat16
    )
    keyvals = jnp.einsum(
        "fnc,cd->fnd",
        normed_all.reshape(frames_core, patch_count * cell_count, C),
        w_keyval,
        preferred_element_type=jnp.float32,
    ).astype(jnp.bfloat16)
    run_max, run_total, run_acc = fold_scores(
        start_carry, queries, keyvals[..., :C], keyvals[..., C:]
    )
    attended = run_acc / run_total[..., None]
    mixed_own = (own_frames.astype(jnp.float32) + attended.reshape(frames_core, RD, W, C)).astype(
        jnp.bfloat16
    )
    mixed = lax.all_gather(mixed_own, "chan", axis=0, tiled=True)
    activated = jax.nn.silu(scaled_rms(mixed)).astype(jnp.bfloat16)
    cached = shifted(activated, "span", 1)
    stacked = jnp.concatenate([cached, activated], axis=0)
    padded = with_halo(stacked, (("patch", 1),), 1)
    padded = jnp.pad(padded, ((0, 0), (0, 0), (1, 1), (0, 0)))
    conv_sum = lax.conv_general_dilated(
        padded[None],
        conv_weight,
        (1, 1, 1),
        "VALID",
        dimension_numbers=("NDHWC", "DHWIO", "NDHWC"),
        preferred_element_type=jnp.float32,
    )[0]
    out_width = conv_weight.shape[-1]
    own_channels = lax.dynamic_slice_in_dim(mixed, chan_index * out_width, out_width, 3)
    return (own_channels.astype(jnp.float32) + conv_sum).astype(jnp.bfloat16)


def solution(mesh):
    placed = (
        P(("clips", "span"), "patch", None, None),
        P(("clips", "span"), None),
        P(),
        P(),
        P(None, None, None, None, "chan"),
    )
    return jax.shard_map(
        local,
        mesh=mesh,
        in_specs=placed,
        out_specs=P(("clips", "span"), "patch", None, "chan"),
        check_vma=False,
    )
```

profile of v0, /device:TPU:0, one launch (start us, length us, event | category | flops | bytes accessed | tf_op | source)
XLA Modules:
  0.0 52.7 jit_solution(9467739739827908105)
XLA Ops:
  0.0 0.0 copy-start
  0.0 0.7 %compare_select_fusion = s32[256,1]{0,1:T(1,128)S(1)} fusion(s32[1,256]{1,0:T(1,128)} %param.6), kind=kLoop, calls=%fused_computation.49 | loop fusion | flops 768 | bytes 2048 | tf_op jit(solution)/shard_map/select_n | solution.py:78
  0.8 1.4 %scatter_custom_fusion = s32[256]{0:T(256)S(1)} fusion(s32[256]{0:T(256)S(1)} %bitcast.54, s32[256]{0:T(256)S(1)} %iota.3, s32[]{:T(128)} %constant.59.clone.1), kind=kCustom, calls=%fused_computation.58 | custom fusion | bytes 1028 | tf_op jit(solution)/shard_map/scatter | solution.py:78
  2.2 0.1 broadcast_in_dim.34
  2.3 0.1 broadcast_in_dim.35
  2.4 0.1 broadcast_in_dim.36
  2.5 21.5 %all_gather.6 = bf16[1,256,4,384]{3,2,0,1:T(4,128)(2,1)S(1)} all-gather(bf16[1,64,4,384]{3,2,0,1:T(4,128)(2,1)} %bitcast.53), channel_id=1, replica_groups=mesh['clips'=2,'patch'=4,'span'=2,'chan'=2] {'patch'}, dimensions={1}, use_global_device_ids=true | all-gather | bytes 983040 | tf_op jit(solution)/shard_map/all_gather | solution.py:75
  24.1 1.5 %gather_fusion = bf16[256,4,384]{2,1,0:T(4,128)(2,1)S(1)} fusion(bf16[256,4,384]{2,1,0:T(4,128)(2,1)S(1)} %bitcast.48, s32[1024]{0:T(1024)S(1)} %pad_clamp_fusion), kind=kCustom, calls=%fused_computation | custom fusion | bytes 1573888 | tf_op jit(solution)/shard_map/jit(_take)/gather | solution.py:80
  25.5 0.2 gather.7
  25.7 0.2 copy_select_fusion
  25.9 0.0 copy-start.1
  25.9 0.2 fusion.14
  26.1 0.2 fusion.15
  26.3 0.0 copy-done
  26.3 0.6 %fusion.2 = bf16[1,512,768]{2,1,0:T(8,128)(2,1)S(1)} fusion(bf16[512,384]{1,0:T(8,128)(2,1)S(1)} %bitcast.49, bf16[384,768]{1,0:T(8,128)(2,1)S(1)} %copy-done), kind=kOutput, calls=%fused_computation.8 | convolution fusion | flops 302383104 | bytes 1769472 | tf_op jit(solution)/shard_map/fnc,cd->fnd/dot_general | solution.py:92
  26.9 0.0 copy-done.1
  26.9 0.5 fusion.31
  27.4 0.2 fusion.20
  27.6 0.3 fusion.3
  27.9 1.9 %all_gather.7 = bf16[2,2,64,384]{3,2,1,0:T(8,128)(2,1)S(1)} all-gather(bf16[1,2,64,384]{3,2,1,0:T(8,128)(2,1)S(1)} %add_convert_fusion), channel_id=1, replica_groups=mesh['clips'=2,'patch'=4,'span'=2,'chan'=2] {'chan'}, dimensions={0}, use_global_device_ids=true | all-gather | bytes 294912 | tf_op jit(solution)/shard_map/all_gather | solution.py:105
  29.9 0.1 fusion.17
  30.0 0.2 multiply_convert_fusion
  30.2 3.4 %collective-permute-start = (bf16[2,2,64,384]{3,2,1,0:T(8,128)(2,1)S(1)}, bf16[2,2,64,384]{3,2,1,0:T(8,128)(2,1)S(1)}, u32[]{:S(2)}, u32[]{:S(2)}) collective-permute-start(bf16[2,2,64,384]{3,2,1,0:T(8,128)(2,1)S(1)} %multiply_convert_fusion), channel_id=1, source_target_pairs={{0,2},{1,3},{4,6},{5,7},{8,10},{9,11},{12,14},{13,15},{16,18},{17,... | collective-permute-start | bytes 589832 | tf_op jit(solution)/shard_map/ppermute | solution.py:20
  33.6 4.4 %collective-permute-done = bf16[2,2,64,384]{3,2,1,0:T(8,128)(2,1)S(1)} collective-permute-done((bf16[2,2,64,384]{3,2,1,0:T(8,128)(2,1)S(1)}, bf16[2,2,64,384]{3,2,1,0:T(8,128)(2,1)S(1)}, u32[]{:S(2)}, u32[]{:S(2)}) %collective-permute-start) | collective-permute-done | bytes 196640 | tf_op jit(solution)/shard_map/ppermute | solution.py:20
  38.1 1.6 %collective-permute-start.1 = (bf16[4,1,64,384]{3,2,1,0:T(8,128)(2,1)S(1)}, bf16[4,1,64,384]{3,2,1,0:T(8,128)(2,1)S(1)}, u32[]{:S(2)}, u32[]{:S(2)}) collective-permute-start(bf16[4,1,64,384]{3,2,1,0:T(8,128)(2,1)S(1)} %get-tuple-element.5), channel_id=1, source_target_pairs={{0,4},{4,8},{8,12},{1,5},{5,9},{9,13},{2,6},{6,10},{10,14},{3,7},{... | collective-permute-start | bytes 589832 | tf_op jit(solution)/shard_map/ppermute | solution.py:31
  39.7 1.3 %collective-permute-start.2 = (bf16[4,1,64,384]{3,2,1,0:T(8,128)(2,1)S(1)}, bf16[4,1,64,384]{3,2,1,0:T(8,128)(2,1)S(1)}, u32[]{:S(2)}, u32[]{:S(2)}) collective-permute-start(bf16[4,1,64,384]{3,2,1,0:T(8,128)(2,1)S(1)} %get-tuple-element.6), channel_id=1, source_target_pairs={{4,0},{8,4},{12,8},{5,1},{9,5},{13,9},{6,2},{10,6},{14,10},{7,3},{... | collective-permute-start | bytes 589832 | tf_op jit(solution)/shard_map/ppermute | solution.py:33
  41.0 0.1 constant_dynamic-slice_fusion
  41.1 2.2 %collective-permute-done.1 = bf16[4,1,64,384]{3,2,1,0:T(8,128)(2,1)S(1)} collective-permute-done((bf16[4,1,64,384]{3,2,1,0:T(8,128)(2,1)S(1)}, bf16[4,1,64,384]{3,2,1,0:T(8,128)(2,1)S(1)}, u32[]{:S(2)}, u32[]{:S(2)}) %collective-permute-start.1) | collective-permute-done | bytes 196640 | tf_op jit(solution)/shard_map/ppermute | solution.py:31
  43.4 4.1 %collective-permute-done.2 = bf16[4,1,64,384]{3,2,1,0:T(8,128)(2,1)S(1)} collective-permute-done((bf16[4,1,64,384]{3,2,1,0:T(8,128)(2,1)S(1)}, bf16[4,1,64,384]{3,2,1,0:T(8,128)(2,1)S(1)}, u32[]{:S(2)}, u32[]{:S(2)}) %collective-permute-start.2) | collective-permute-done | bytes 196640 | tf_op jit(solution)/shard_map/ppermute | solution.py:33
  47.5 0.3 fusion.10
  47.8 0.0 copy-start.2
  47.8 0.3 copy.34
  48.1 0.0 copy-start.3
  48.2 0.3 pad.5.clone
  48.5 0.1 copy.30
  48.6 0.1 slice.24
  48.7 1.3 %copy-done.2 = bf16[3,3,3,384,192]{3,4,2,1,0:T(8,128)(2,1)S(1)} copy-done((bf16[3,3,3,384,192]{3,4,2,1,0:T(8,128)(2,1)S(1)}, bf16[3,3,3,384,192]{3,4,2,1,0:T(8,128)(2,1)}, u32[]{:S(2)}) %copy-start.2) | copy-done | bytes 3981336
  49.9 0.0 copy-done.3
  49.9 1.8 %convolution_select_fusion = f32[2,2,8,9,192]{4,2,3,1,0:T(8,128)S(1)} fusion(bf16[3,3,3,384,192]{3,4,2,1,0:T(8,128)(2,1)S(1)} %copy-done.2, bf16[4,4,1,7,2,384]{5,3,4,1,0,2:T(8,128)(2,1)S(1)} %slice.24, bf16[4,4,1,8,9,384]{5,3,4,1,0,2:T(8,128)(2,1)S(1)} %copy.30, pred[8,9]{0,1:T(8,128)(4,1)S(1)} %copy-done.3), kind=kOutput, calls=%fused_computation.10 | convolution fusion | flops 1149917184 | bytes 5259336 | tf_op jit(solution)/shard_map/conv_general_dilated | solution.py:111
  51.7 0.2 copy.31
  51.9 0.2 fusion.19
  52.0 0.7 %copy.32 = bf16[2,2,64,192]{3,2,1,0:T(8,128)(2,1)} copy(bf16[2,2,64,192]{3,1,2,0:T(2,128)(2,1)S(1)} %fusion.19) | data formatting | bytes 196608 | tf_op jit(solution)/shard_map/convert_element_type | solution.py:121
  (12 shorter events, 0.2 us)
Async XLA Ops:
  0.0 26.3 %copy-start = (bf16[384,768]{1,0:T(8,128)(2,1)S(1)}, bf16[384,768]{1,0:T(8,128)(2,1)}, u32[]{:S(2)}) copy-start(bf16[384,768]{1,0:T(8,128)(2,1)} %param.8) | copy-start | bytes 1769476
  25.9 1.0 %copy-start.1 = (bf16[384,384]{1,0:T(8,128)(2,1)S(1)}, bf16[384,384]{1,0:T(8,128)(2,1)}, u32[]{:S(2)}) copy-start(bf16[384,384]{1,0:T(8,128)(2,1)} %param.7) | copy-start | bytes 884740
  30.2 7.9 %collective-permute-start = (bf16[2,2,64,384]{3,2,1,0:T(8,128)(2,1)S(1)}, bf16[2,2,64,384]{3,2,1,0:T(8,128)(2,1)S(1)}, u32[]{:S(2)}, u32[]{:S(2)}) collective-permute-start(bf16[2,2,64,384]{3,2,1,0:T(8,128)(2,1)S(1)} %multiply_convert_fusion), channel_id=1, source_target_pairs={{0,2},{1,3},{4,6},{5,7},{8,10},{9,11},{12,14},{13,15},{16,18},{17,... | collective-permute-start | bytes 589832 | tf_op jit(solution)/shard_map/ppermute | solution.py:20
  38.1 5.2 %collective-permute-start.1 = (bf16[4,1,64,384]{3,2,1,0:T(8,128)(2,1)S(1)}, bf16[4,1,64,384]{3,2,1,0:T(8,128)(2,1)S(1)}, u32[]{:S(2)}, u32[]{:S(2)}) collective-permute-start(bf16[4,1,64,384]{3,2,1,0:T(8,128)(2,1)S(1)} %get-tuple-element.5), channel_id=1, source_target_pairs={{0,4},{4,8},{8,12},{1,5},{5,9},{9,13},{2,6},{6,10},{10,14},{3,7},{... | collective-permute-start | bytes 589832 | tf_op jit(solution)/shard_map/ppermute | solution.py:31
  39.7 7.8 %collective-permute-start.2 = (bf16[4,1,64,384]{3,2,1,0:T(8,128)(2,1)S(1)}, bf16[4,1,64,384]{3,2,1,0:T(8,128)(2,1)S(1)}, u32[]{:S(2)}, u32[]{:S(2)}) collective-permute-start(bf16[4,1,64,384]{3,2,1,0:T(8,128)(2,1)S(1)} %get-tuple-element.6), channel_id=1, source_target_pairs={{4,0},{8,4},{12,8},{5,1},{9,5},{13,9},{6,2},{10,6},{14,10},{7,3},{... | collective-permute-start | bytes 589832 | tf_op jit(solution)/shard_map/ppermute | solution.py:33
  47.8 2.1 %copy-start.2 = (bf16[3,3,3,384,192]{3,4,2,1,0:T(8,128)(2,1)S(1)}, bf16[3,3,3,384,192]{3,4,2,1,0:T(8,128)(2,1)}, u32[]{:S(2)}) copy-start(bf16[3,3,3,384,192]{3,4,2,1,0:T(8,128)(2,1)} %param.9) | copy-start | bytes 11943940
  48.1 1.8 %copy-start.3 = (pred[8,9]{0,1:T(8,128)(4,1)S(1)}, pred[8,9]{0,1:T(8,128)(4,1)}, u32[]{:S(2)}) copy-start(pred[8,9]{0,1:T(8,128)(4,1)} %constant.87) | copy-start | bytes 220
where the time goes:
time: 53 us; the launch traced here: 52.7 us
  blocking collectives  23.5 us (44%)
  waiting for transfers between devices  10.8 us (20%)
  local copies, waits for them, and re-layouts  6.42 us (12%)
  starting transfers between devices  6.26 us (12%)
  matrix products  3.09 us (6%)
  other arithmetic  2.41 us (5%)
    all_gather x1, blocking collectives, local(): every_tile = lax.all_gather(latent_tiles, 'patch', axis=1, tiled=True)[0]  21.5 us
    ppermute x1, waiting for transfers between devices, shifted(): return lax.ppermute(x, axis, pairs)  4.45 us
    ppermute x1, waiting for transfers between devices, with_halo(): lax.ppermute(head, axis, [((i + 1) % count, i) for i in range(ends)])  4.12 us
    ppermute x1, starting transfers between devices, shifted(): return lax.ppermute(x, axis, pairs)  3.41 us
    ppermute x1, waiting for transfers between devices, with_halo(): lax.ppermute(tail, axis, [(i, (i + 1) % count) for i in range(ends)])  2.23 us
    all_gather x1, blocking collectives, local(): mixed = lax.all_gather(mixed_own, 'chan', axis=0, tiled=True)  1.95 us
    conv_general_dilated x1, matrix products, local(): lax.conv_general_dilated(padded[None], conv_weight, (1, 1, 1), 'VALID', d...  1.75 us
    gather x2, local copies, waits for them, and re-layouts, local(): jnp.take(every_tile, inverse, axis=0).reshape(patch_count, FD, RD, W, C)  1.65 us
  transfers between devices with their start and end apart: 3, of which 3 were waited for; matrix products, arithmetic and copies ran while one was open for 0% of the time, Pallas kernels for 0%

commit v1 on v0

v1 whole, which is shorter than its diff:
```python
import functools
import math

import jax
import jax.numpy as jnp
from jax import lax
from jax.experimental import pallas as pl
from jax.experimental.pallas import tpu as pltpu
from jax.sharding import PartitionSpec as P

C = 384
W = 64
RD = 2
FD = 2
CELLS = FD * RD * W
HALO = FD * (RD + 2) * W
PIECES = 2
KEY_BLOCK = 1024

epsilon = 1e-06
MESH = pl.DeviceIdType.MESH


def scaled_rms(wide):
    return wide / jnp.sqrt(jnp.mean(wide * wide, axis=-1, keepdims=True) + epsilon)


def block_kernel(
    patches,
    spans,
    tiles_ref,
    keys_ref,
    w_query_ref,
    w_keyval_ref,
    conv_ref,
    out_ref,
    tiles,
    keyvals,
    gathered,
    shifted3,
    mixed,
    total,
    w_query,
    w_keyval,
    conv,
    ahead,
    behind,
    load_sem,
    right_send,
    right_recv,
    left_send,
    left_recv,
    pair_send,
    pair_recv,
    span_send,
    span_recv,
):
    z = lax.axis_index("patch")
    x = lax.axis_index("span")
    core = lax.axis_index("chan")
    other = 1 - core
    half = CELLS // 2
    piece = half // PIECES
    band = RD * W

    own_load = pltpu.make_async_copy(tiles_ref, tiles.at[z], load_sem.at[0])
    own_load.start()
    keyval_load = pltpu.make_async_copy(w_keyval_ref, w_keyval, load_sem.at[1])
    keyval_load.start()
    query_load = pltpu.make_async_copy(w_query_ref, w_query, load_sem.at[2])
    query_load.start()
    conv_load = pltpu.make_async_copy(conv_ref, conv, load_sem.at[3])
    conv_load.start()

    barrier = pltpu.get_barrier_semaphore()

    def greet(near, target):
        @pl.when(near)
        def _():
            pl.semaphore_signal(barrier, inc=1, device_id=target, device_id_type=MESH)

    has_left, has_right = z > 0, z < patches - 1
    has_before, has_after = x > 0, x < spans - 1
    greet(has_left, {"patch": z - 1})
    greet(has_right, {"patch": z + 1})
    greet(has_before, {"span": x - 1})
    greet(has_after, {"span": x + 1})
    pl.semaphore_signal(barrier, inc=1, device_id={"chan": other}, device_id_type=MESH)
    near_count = (
        1
        + jnp.where(has_left, 1, 0)
        + jnp.where(has_right, 1, 0)
        + jnp.where(has_before, 1, 0)
        + jnp.where(has_after, 1, 0)
    )
    pl.semaphore_wait(barrier, near_count)

    def part(origin, side, k):
        return tiles.at[origin, pl.ds(pl.multiple_of(side * half + k * piece, piece), piece)]

    def send_right(origin, k):
        return pltpu.make_async_remote_copy(
            part(origin, core, k),
            part(origin, core, k),
            right_send.at[origin, k],
            right_recv.at[origin, k],
            device_id={"patch": z + 1},
            device_id_type=MESH,
        )

    def send_left(origin, k):
        return pltpu.make_async_remote_copy(
            part(origin, core, k),
            part(origin, core, k),
            left_send.at[origin, k],
            left_recv.at[origin, k],
            device_id={"patch": z - 1},
            device_id_type=MESH,
        )

    def send_pair(origin, side, k):
        return pltpu.make_async_remote_copy(
            part(origin, side, k),
            part(origin, side, k),
            pair_send.at[origin, k],
            pair_recv.at[origin, k],
            device_id={"chan": other},
            device_id_type=MESH,
        )

    def when(condition, action):
        @pl.when(condition)
        def _():
            action()

    own_load.wait()
    for k in range(PIECES):
        when(has_right, lambda: send_right(z, k).start())
        when(has_left, lambda: send_left(z, k).start())

    at = lax.broadcasted_iota(jnp.int32, (HALO, 1), 0)
    frame = at // ((RD + 2) * W)
    row = z * RD - 1 + (at // W) % (RD + 2)
    owner = (row + RD) // RD - 1
    wanted = owner * CELLS + (frame * RD + (row + RD) % RD) * W + at % W

    def absorb(origin):
        values = tiles[origin]
        normed = scaled_rms(values.astype(jnp.float32)).astype(jnp.bfloat16)
        keyvals[origin] = jnp.dot(
            normed, w_keyval[...], preferred_element_type=jnp.float32
        ).astype(jnp.bfloat16)
        picks = jnp.where(keys_ref[origin] == wanted, 1.0, 0.0).astype(jnp.bfloat16)
        gathered[...] += jnp.dot(picks, values, preferred_element_type=jnp.float32)

    gathered[...] = jnp.zeros_like(gathered)
    keyval_load.wait()
    absorb(z)

    def absorb_step(step):
        def from_pair(origin):
            for k in range(PIECES):
                send_pair(origin, other, k).wait_recv()
            absorb(origin)

        when(z - step >= 0, lambda: from_pair(z - step))
        when(z + step < patches, lambda: from_pair(z + step))

    def pass_on(step):
        for k in range(PIECES):

            def from_left():
                origin = z - step
                send_right(origin, k).wait_recv()
                when(has_right, lambda: send_right(origin, k).start())
                send_pair(origin, core, k).start()

            def from_right():
                origin = z + step
                send_left(origin, k).wait_recv()
                when(has_left, lambda: send_left(origin, k).start())
                send_pair(origin, core, k).start()

            when(z - step >= 0, from_left)
            when(z + step < patches, from_right)

    pass_on(1)

    def gather_step(step, carry):
        pass_on(step)
        absorb_step(step - 1)
        return carry

    lax.fori_loop(2, patches, gather_step, 0)
    absorb_step(patches - 1)

    query_load.wait()
    queries = jnp.dot(
        scaled_rms(gathered[...]).astype(jnp.bfloat16),
        w_query[...],
        preferred_element_type=jnp.float32,
    ).astype(jnp.bfloat16)
    scale = 1.0 / math.sqrt(C)
    group = min(KEY_BLOCK // CELLS, patches)
    frame_cells = HALO // FD

    def fold(block, carry, f):
        run_max, run_total, run_acc = carry
        first = block * group
        pair = keyvals[pl.ds(first, group)].reshape(group * CELLS, 2 * C)
        codes = keys_ref[pl.ds(first, group)]
        allow = (codes // (RD * W)) % FD == f
        bias = jnp.where(allow, 0.0, -1e30)
        bias = jnp.concatenate([bias[j] for j in range(group)], axis=-1)
        scores = lax.dot_general(
            queries[f * frame_cells : (f + 1) * frame_cells],
            pair[:, :C],
            (((1,), (1,)), ((), ())),
            preferred_element_type=jnp.float32,
        )
        scores = scores * scale + bias
        top = jnp.max(scores, axis=-1, keepdims=True)
        if run_max is not None:
            top = jnp.maximum(top, run_max)
        powers = jnp.exp(scores - top)
        sums = jnp.sum(powers, axis=-1, keepdims=True)
        acc = jnp.dot(
            powers.astype(jnp.bfloat16), pair[:, C:], preferred_element_type=jnp.float32
        )
        if run_max is not None:
            factor = jnp.exp(run_max - top)
            sums = run_total * factor + sums
            acc = run_acc * factor + acc
        return top, sums, acc

    line = lax.broadcasted_iota(jnp.int32, (frame_cells, 1), 0)
    line_row = z * RD - 1 + line // W
    inside = (line_row >= 0) & (line_row < patches * RD)
    for f in range(FD):
        span_of = slice(f * frame_cells, (f + 1) * frame_cells)
        carry = fold(0, (None, None, None), f)
        if patches > group:
            carry = lax.fori_loop(
                1, patches // group, functools.partial(fold, f=f), carry
            )
        _, sums, acc = carry
        rounded = (gathered[span_of] + acc / sums).astype(jnp.bfloat16)
        mixed[span_of] = rounded
        v = scaled_rms(rounded.astype(jnp.float32))
        act = jnp.where(inside, v / (1.0 + jnp.exp(-v)), 0.0)
        before = jnp.where(line % W == 0, 0.0, pltpu.roll(act, 1, 0))
        after = jnp.where(line % W == W - 1, 0.0, pltpu.roll(act, frame_cells - 1, 0))
        shifted3[span_of, 0:C] = before.astype(jnp.bfloat16)
        shifted3[span_of, C : 2 * C] = act.astype(jnp.bfloat16)
        shifted3[span_of, 2 * C : 3 * C] = after.astype(jnp.bfloat16)

    def rows_of(ref, b):
        return jnp.concatenate(
            [ref[f * frame_cells + b * W : f * frame_cells + b * W + band] for f in range(FD)],
            axis=0,
        )

    def conv_time(a):
        result = None
        for b in range(3):
            term = jnp.dot(
                rows_of(shifted3, b), conv[3 * a + b], preferred_element_type=jnp.float32
            )
            result = term if result is None else result + term
        return result

    def send_span(t):
        return pltpu.make_async_remote_copy(
            ahead.at[t],
            behind.at[t],
            span_send.at[t],
            span_recv.at[t],
            device_id={"span": x + 1},
            device_id_type=MESH,
        )

    conv_load.wait()
    oldest = conv_time(0)
    ahead[1] = oldest[band:].astype(jnp.bfloat16)
    when(has_after, lambda: send_span(1).start())
    middle = conv_time(1)
    ahead[0] = (oldest[:band] + middle[band:]).astype(jnp.bfloat16)
    when(has_after, lambda: send_span(0).start())
    width = out_ref.shape[-1]
    pick_from = lax.broadcasted_iota(jnp.int32, (C, width), 0)
    pick_to = lax.broadcasted_iota(jnp.int32, (C, width), 1) + core * width
    picks = jnp.where(pick_from == pick_to, 1.0, 0.0).astype(jnp.bfloat16)
    newest = conv_time(2) + jnp.dot(
        rows_of(mixed, 1), picks, preferred_element_type=jnp.float32
    )
    total[0:band] = newest[:band]
    total[band : 2 * band] = newest[band:] + middle[:band]

    @pl.when(x == 0)
    def _():
        out_ref[...] = total[...].astype(jnp.bfloat16)

    @pl.when(has_before)
    def _():
        for t in range(FD):
            send_span(t).wait_recv()
            here = slice(t * band, (t + 1) * band)
            out_ref[here] = (total[here] + behind[t].astype(jnp.float32)).astype(jnp.bfloat16)

    @pl.when(has_after)
    def _():
        for t in range(FD):
            send_span(t).wait_send()

    def finish(step, carry):
        for k in range(PIECES):

            def left_origin():
                when(has_right, lambda: send_right(z - step, k).wait_send())
                when(step > 0, lambda: send_pair(z - step, core, k).wait_send())

            def right_origin():
                when(has_left, lambda: send_left(z + step, k).wait_send())
                when(step > 0, lambda: send_pair(z + step, core, k).wait_send())

            when(z - step >= 0, left_origin)
            when(z + step < patches, right_origin)
        return carry

    lax.fori_loop(0, patches, finish, 0)


def local(latent_tiles, route, w_query, w_keyval, conv_weight):
    patches = lax.axis_size("patch")
    spans = lax.axis_size("span")
    width = conv_weight.shape[-1]
    tiles_own = latent_tiles.reshape(CELLS, C)
    tile_cells = latent_tiles.shape[2]
    keys = (
        route.reshape(patches, -1, 1) * tile_cells + jnp.arange(tile_cells, dtype=jnp.int32)
    ).reshape(patches, 1, CELLS)
    bf16, f32 = jnp.bfloat16, jnp.float32
    dma = pltpu.SemaphoreType.DMA
    anywhere = pl.BlockSpec(memory_space=pl.ANY)
    vmem = pl.BlockSpec(memory_space=pltpu.VMEM)
    result = pl.pallas_call(
        functools.partial(block_kernel, patches, spans),
        out_shape=jax.ShapeDtypeStruct((FD * RD * W, width), bf16),
        in_specs=[anywhere, vmem, anywhere, anywhere, anywhere],
        out_specs=vmem,
        scratch_shapes=[
            pltpu.VMEM((patches, CELLS, C), bf16),
            pltpu.VMEM((patches, CELLS, 2 * C), bf16),
            pltpu.VMEM((HALO, C), f32),
            pltpu.VMEM((HALO, 3 * C), bf16),
            pltpu.VMEM((HALO, C), bf16),
            pltpu.VMEM((FD * RD * W, width), f32),
            pltpu.VMEM((C, C), bf16),
            pltpu.VMEM((C, 2 * C), bf16),
            pltpu.VMEM((9, 3 * C, width), bf16),
            pltpu.VMEM((FD, RD * W, width), bf16),
            pltpu.VMEM((FD, RD * W, width), bf16),
            dma((4,)),
            dma((patches, PIECES)),
            dma((patches, PIECES)),
            dma((patches, PIECES)),
            dma((patches, PIECES)),
            dma((patches, PIECES)),
            dma((patches, PIECES)),
            dma((FD,)),
            dma((FD,)),
        ],
        compiler_params=pltpu.CompilerParams(
            collective_id=0, has_side_effects=True, vmem_limit_bytes=56 * 1024 * 1024
        ),
    )(tiles_own, keys, w_query, w_keyval, conv_weight.reshape(9, 3 * C, width))
    return result.reshape(FD, RD, W, width)


def solution(mesh):
    placed = (
        P(("clips", "span"), "patch", None, None),
        P(("clips", "span"), None),
        P(),
        P(),
        P(None, None, None, None, "chan"),
    )
    return jax.shard_map(
        local,
        mesh=mesh,
        in_specs=placed,
        out_specs=P(("clips", "span"), "patch", None, "chan"),
        check_vma=False,
    )
```

time: 53 us -> 39.6 us (0.75)
  Pallas kernels: 0 us -> 26.1 us
  blocking collectives: 23.5 us -> 0 us
  waiting for transfers between devices: 10.8 us -> 0 us
  starting transfers between devices: 6.26 us -> 0 us
  local copies, waits for them, and re-layouts: 6.42 us -> 11.8 us
  matrix products: 3.09 us -> 0 us
  other arithmetic: 2.41 us -> 1.3 us
    pallas_call x0 -> x1, Pallas kernels: none -> 26.1 us  [local(): pl.pallas_call(functools.partial(block_kernel, patches, spans), out_shape...]
    all_gather x2 -> x0, blocking collectives: 23.5 us -> none  [the longest x1 21.5 us: local(): every_tile = lax.all_gather(latent_tiles, 'patch', axis=1, tiled=True)[0]]
    ppermute x3 -> x0, waiting for transfers between devices: 10.8 us -> none  [the longest x1 4.45 us: shifted(): return lax.ppermute(x, axis, pairs)]
    unnamed x9 -> x2, local copies, waits for them, and re-layouts: 1.61 us -> 9.73 us
    ppermute x3 -> x0, starting transfers between devices: 6.26 us -> none  [the longest x1 3.41 us: shifted(): return lax.ppermute(x, axis, pairs)]
    conv_general_dilated x1 -> x0, matrix products: 1.75 us -> none  [local(): lax.conv_general_dilated(padded[None], conv_weight, (1, 1, 1), 'VALID', d...]
    gather x2 -> x0, local copies, waits for them, and re-layouts: 1.65 us -> none  [local(): jnp.take(every_tile, inverse, axis=0).reshape(patch_count, FD, RD, W, C)]
    reshape x0 -> x1, local copies, waits for them, and re-layouts: none -> 1.65 us  [local(): tiles_own = latent_tiles.reshape(CELLS, C)]
  transfers between devices with their start and end apart: 3 -> 0, of which waited for: 3 -> 0; matrix products, arithmetic and copies ran while one was open for 0% -> 0% of each run, Pallas kernels for 0% -> 0%
where the time goes in v1:
time: 39.6 us; the launch traced here: 39.3 us
  Pallas kernels  26.1 us (66%)
  local copies, waits for them, and re-layouts  11.8 us (30%)
  other arithmetic  1.3 us (3%)
    pallas_call x1, Pallas kernels, local(): pl.pallas_call(functools.partial(block_kernel, patches, spans), out_shape...  26.1 us
    unnamed x2, local copies, waits for them, and re-layouts  9.73 us
    reshape x1, local copies, waits for them, and re-layouts, local(): tiles_own = latent_tiles.reshape(CELLS, C)  1.65 us

profile of v1, /device:TPU:0, one launch (start us, length us, event | category | flops | bytes accessed | tf_op | source)
XLA Modules:
  0.0 39.3 jit_solution(2401373188593867355)
XLA Ops:
  0.0 0.7 %multiply_reduce_fusion = s32[256]{0:T(256)S(1)} fusion(s32[1,256]{1,0:T(1,128)} %param.6), kind=kLoop, calls=%fused_computation.1 | loop fusion | flops 256 | bytes 2048 | tf_op jit(solution)/shard_map/mul | solution.py:340
  0.7 0.1 mul.16
  0.8 0.1 add.29
  0.9 0.1 add.26
  1.0 0.1 add.32
  1.1 0.6 %broadcast_add_fusion.keys_ref = s32[4,1,256]{2,1,0:T(1,128)} fusion(s32[4,1,256]{2,1,0:T(1,128)S(1)} %add.32, s32[256]{0:T(256)S(1)} %add.29), kind=kLoop, calls=%fused_computation | loop fusion | flops 1024 | bytes 9216 | tf_op jit(solution)/shard_map/add | solution.py:340
  1.7 1.6 %reshape.54.tiles_ref = bf16[256,384]{1,0:T(8,128)(2,1)} reshape(bf16[1,64,4,384]{3,2,1,0:T(4,128)(2,1)} %param.5) | data formatting | bytes 393216 | tf_op jit(solution)/shard_map/reshape | solution.py:337
  3.4 8.2 %copy.11 = bf16[3,3,3,384,192]{4,3,2,1,0:T(8,128)(2,1)} copy(bf16[3,3,3,384,192]{3,4,2,1,0:T(8,128)(2,1)} %param.9) | data formatting | bytes 7962624 | tf_op args[4]
  11.5 26.1 %shard_map.55 = bf16[256,192]{1,0:T(8,128)(2,1)} custom-call(bf16[256,384]{1,0:T(8,128)(2,1)} %reshape.54.tiles_ref, s32[4,1,256]{2,1,0:T(1,128)} %broadcast_add_fusion.keys_ref, bf16[384,384]{1,0:T(8,128)(2,1)} %w_query_ref.1, bf16[384,768]{1,0:T(8,128)(2,1)} %w_keyval_ref.1, bf16[9,1152,192]{2,1,0:T(8,128)(2,1)} %bitcast.2), custom_call_target="tpu_custom_call" | custom-call | tf_op jit(solution)/shard_map/pallas_call | solution.py:346
  37.7 1.6 %copy.13 = bf16[2,2,64,192]{3,2,1,0:T(8,128)(2,1)} copy(bf16[2,2,64,192]{3,2,1,0:T(8,128)(2,1)} %bitcast.3) | data formatting | bytes 196608
  (1 shorter events, 0.0 us)

commit v2 on v1

--- a/solution.py
+++ b/solution.py
@@ -29,11 +29,14 @@
     patches,
     spans,
     tiles_ref,
-    keys_ref,
+    route_ref,
     w_query_ref,
     w_keyval_ref,
     conv_ref,
     out_ref,
+    raw,
+    places_of,
+    keys_ref,
     tiles,
     keyvals,
     gathered,
@@ -63,16 +66,19 @@
     piece = half // PIECES
     band = RD * W
 
-    own_load = pltpu.make_async_copy(tiles_ref, tiles.at[z], load_sem.at[0])
+    own_load = pltpu.make_async_copy(tiles_ref, raw, load_sem.at[0])
     own_load.start()
     keyval_load = pltpu.make_async_copy(w_keyval_ref, w_keyval, load_sem.at[1])
     keyval_load.start()
+    route_load = pltpu.make_async_copy(route_ref, places_of, load_sem.at[4])
+    route_load.start()
     query_load = pltpu.make_async_copy(w_query_ref, w_query, load_sem.at[2])
     query_load.start()
     conv_load = pltpu.make_async_copy(conv_ref, conv, load_sem.at[3])
     conv_load.start()
 
     barrier = pltpu.get_barrier_semaphore()
+    here, tile_cells = raw.shape[0], raw.shape[1]
 
     def greet(near, target):
         @pl.when(near)
@@ -134,6 +140,7 @@
             action()
 
     own_load.wait()
+    tiles[z] = raw[...].reshape(CELLS, C)
     for k in range(PIECES):
         when(has_right, lambda: send_right(z, k).start())
         when(has_left, lambda: send_left(z, k).start())
@@ -152,6 +159,27 @@
         ).astype(jnp.bfloat16)
         picks = jnp.where(keys_ref[origin] == wanted, 1.0, 0.0).astype(jnp.bfloat16)
         gathered[...] += jnp.dot(picks, values, preferred_element_type=jnp.float32)
+
+    lanes = 2 * here
+    spread_from = lax.broadcasted_iota(jnp.int32, (lanes, 2 * CELLS), 0)
+    spread_to = lax.broadcasted_iota(jnp.int32, (lanes, 2 * CELLS), 1)
+    spread = jnp.where(spread_to // tile_cells == spread_from, 1.0, 0.0).astype(jnp.bfloat16)
+    cell = lax.broadcasted_iota(jnp.int32, (1, 2 * CELLS), 1) % tile_cells
+    route_load.wait()
+    for j in range(patches // 2):
+        places = places_of[:, j * lanes : (j + 1) * lanes]
+        digits = jnp.concatenate(
+            [jnp.broadcast_to(d, (8, lanes)) for d in (places // 256, places % 256)], axis=0
+        )
+        wide = jnp.dot(
+            digits.astype(jnp.float32).astype(jnp.bfloat16),
+            spread,
+            preferred_element_type=jnp.float32,
+        )
+        place = (wide[0:1] * 256.0 + wide[8:9]).astype(jnp.int32)
+        codes = place * tile_cells + cell
+        keys_ref[2 * j] = codes[:, :CELLS]
+        keys_ref[2 * j + 1] = codes[:, CELLS:]
 
     gathered[...] = jnp.zeros_like(gathered)
     keyval_load.wait()
@@ -263,8 +291,13 @@
     def conv_time(a):
         result = None
         for b in range(3):
-            term = jnp.dot(
-                rows_of(shifted3, b), conv[3 * a + b], preferred_element_type=jnp.float32
+            at_tap = 3 * (3 * a + b)
+            weights = jnp.concatenate([conv[at_tap + c] for c in range(3)], axis=-1)
+            term = lax.dot_general(
+                rows_of(shifted3, b),
+                weights,
+                (((1,), (1,)), ((), ())),
+                preferred_element_type=jnp.float32,
             )
             result = term if result is None else result + term
         return result
@@ -334,21 +367,20 @@
     patches = lax.axis_size("patch")
     spans = lax.axis_size("span")
     width = conv_weight.shape[-1]
-    tiles_own = latent_tiles.reshape(CELLS, C)
-    tile_cells = latent_tiles.shape[2]
-    keys = (
-        route.reshape(patches, -1, 1) * tile_cells + jnp.arange(tile_cells, dtype=jnp.int32)
-    ).reshape(patches, 1, CELLS)
+    tiles_here, tile_cells = latent_tiles.shape[1:3]
     bf16, f32 = jnp.bfloat16, jnp.float32
     dma = pltpu.SemaphoreType.DMA
     anywhere = pl.BlockSpec(memory_space=pl.ANY)
     vmem = pl.BlockSpec(memory_space=pltpu.VMEM)
     result = pl.pallas_call(
         functools.partial(block_kernel, patches, spans),
-        out_shape=jax.ShapeDtypeStruct((FD * RD * W, width), bf16),
-        in_specs=[anywhere, vmem, anywhere, anywhere, anywhere],
+        out_shape=pltpu.VMEM((FD * RD * W, width), bf16),
+        in_specs=[anywhere] * 5,
         out_specs=vmem,
         scratch_shapes=[
+            pltpu.VMEM((tiles_here, tile_cells, C), bf16),
+            pltpu.VMEM(route.shape, jnp.int32),
+            pltpu.VMEM((patches, 1, CELLS), jnp.int32),
             pltpu.VMEM((patches, CELLS, C), bf16),
             pltpu.VMEM((patches, CELLS, 2 * C), bf16),
             pltpu.VMEM((HALO, C), f32),
@@ -357,10 +389,10 @@
             pltpu.VMEM((FD * RD * W, width), f32),
             pltpu.VMEM((C, C), bf16),
             pltpu.VMEM((C, 2 * C), bf16),
-            pltpu.VMEM((9, 3 * C, width), bf16),
+            pltpu.VMEM((27, width, C), bf16),
             pltpu.VMEM((FD, RD * W, width), bf16),
             pltpu.VMEM((FD, RD * W, width), bf16),
-            dma((4,)),
+            dma((5,)),
             dma((patches, PIECES)),
             dma((patches, PIECES)),
             dma((patches, PIECES)),
@@ -373,7 +405,13 @@
         compiler_params=pltpu.CompilerParams(
             collective_id=0, has_side_effects=True, vmem_limit_bytes=56 * 1024 * 1024
         ),
-    )(tiles_own, keys, w_query, w_keyval, conv_weight.reshape(9, 3 * C, width))
+    )(
+        latent_tiles.reshape(tiles_here, tile_cells, C),
+        route,
+        w_query,
+        w_keyval,
+        conv_weight.transpose(0, 1, 2, 4, 3).reshape(27, width, C),
+    )
     return result.reshape(FD, RD, W, width)
 
 

time: 39.6 us -> 25.8 us (0.65)
  local copies, waits for them, and re-layouts: 11.8 us -> 0.66 us
  other arithmetic: 1.3 us -> 0 us
  Pallas kernels: 26.1 us -> 25 us
    unnamed x2 -> x1, local copies, waits for them, and re-layouts: 9.73 us -> 0.66 us
    reshape x1 -> x0, local copies, waits for them, and re-layouts: 1.65 us -> none  [local(): tiles_own = latent_tiles.reshape(CELLS, C)]
    pallas_call x1, Pallas kernels: 26.1 us -> 25 us  [local(): pl.pallas_call(functools.partial(block_kernel, patches, spans), out_shape...]
    mul x1 -> x0, other arithmetic: 0.7 us -> none  [local(): route.reshape(patches, -1, 1) * tile_cells]
    add x1 -> x0, other arithmetic: 0.6 us -> none  [local(): route.reshape(patches, -1, 1) * tile_cells]
where the time goes in v2:
time: 25.8 us; the launch traced here: 25.7 us
  Pallas kernels  25 us (97%)
  local copies, waits for them, and re-layouts  0.66 us (3%)
    pallas_call x1, Pallas kernels, local(): pl.pallas_call(functools.partial(block_kernel, patches, spans), out_shape...  25 us
    unnamed x1, local copies, waits for them, and re-layouts  0.66 us

profile of v2, /device:TPU:0, one launch (start us, length us, event | category | flops | bytes accessed | tf_op | source)
XLA Modules:
  0.0 25.7 jit_solution(3601212438575953394)
XLA Ops:
  0.0 25.0 %shard_map.55 = bf16[256,192]{1,0:T(8,128)(2,1)S(1)} custom-call(bf16[64,4,384]{2,1,0:T(4,128)(2,1)} %bitcast.7, s32[1,256]{1,0:T(1,128)} %route_ref.1, bf16[384,384]{1,0:T(8,128)(2,1)} %w_query_ref.1, bf16[384,768]{1,0:T(8,128)(2,1)} %w_keyval_ref.1, bf16[27,192,384]{2,1,0:T(8,128)(2,1)} %bitcast.6), custom_call_target="tpu_custom_call" | custom-call | tf_op jit(solution)/shard_map/pallas_call | solution.py:375
  25.0 0.7 %copy.7 = bf16[2,2,64,192]{3,2,1,0:T(8,128)(2,1)} copy(bf16[2,2,64,192]{3,2,1,0:T(8,128)(2,1)S(1)} %bitcast.5) | data formatting | bytes 196608

commit v3 on v2

--- a/solution.py
+++ b/solution.py
@@ -34,7 +34,6 @@
     w_keyval_ref,
     conv_ref,
     out_ref,
-    raw,
     places_of,
     keys_ref,
     tiles,
@@ -62,11 +61,27 @@
     x = lax.axis_index("span")
     core = lax.axis_index("chan")
     other = 1 - core
-    half = CELLS // 2
+    half = tiles.shape[1] // 2
     piece = half // PIECES
     band = RD * W
 
-    own_load = pltpu.make_async_copy(tiles_ref, raw, load_sem.at[0])
+    barrier = pltpu.get_barrier_semaphore()
+    here, tile_cells = tiles.shape[1], tiles.shape[2]
+
+    def greet(near, target):
+        @pl.when(near)
+        def _():
+            pl.semaphore_signal(barrier, inc=1, device_id=target, device_id_type=MESH)
+
+    has_left, has_right = z > 0, z < patches - 1
+    has_before, has_after = x > 0, x < spans - 1
+    greet(has_left, {"patch": z - 1})
+    greet(has_right, {"patch": z + 1})
+    greet(has_before, {"span": x - 1})
+    greet(has_after, {"span": x + 1})
+    pl.semaphore_signal(barrier, inc=1, device_id={"chan": other}, device_id_type=MESH)
+
+    own_load = pltpu.make_async_copy(tiles_ref, tiles.at[z], load_sem.at[0])
     own_load.start()
     keyval_load = pltpu.make_async_copy(w_keyval_ref, w_keyval, load_sem.at[1])
     keyval_load.start()
@@ -77,21 +92,6 @@
     conv_load = pltpu.make_async_copy(conv_ref, conv, load_sem.at[3])
     conv_load.start()
 
-    barrier = pltpu.get_barrier_semaphore()
-    here, tile_cells = raw.shape[0], raw.shape[1]
-
-    def greet(near, target):
-        @pl.when(near)
-        def _():
-            pl.semaphore_signal(barrier, inc=1, device_id=target, device_id_type=MESH)
-
-    has_left, has_right = z > 0, z < patches - 1
-    has_before, has_after = x > 0, x < spans - 1
-    greet(has_left, {"patch": z - 1})
-    greet(has_right, {"patch": z + 1})
-    greet(has_before, {"span": x - 1})
-    greet(has_after, {"span": x + 1})
-    pl.semaphore_signal(barrier, inc=1, device_id={"chan": other}, device_id_type=MESH)
     near_count = (
         1
         + jnp.where(has_left, 1, 0)
@@ -102,11 +102,14 @@
     pl.semaphore_wait(barrier, near_count)
 
     def part(origin, side, k):
-        return tiles.at[origin, pl.ds(pl.multiple_of(side * half + k * piece, piece), piece)]
-
-    def send_right(origin, k):
+        return tiles.at[origin, pl.ds(side * half + k * piece, piece)]
+
+    def own_part(k):
+        return tiles_ref.at[pl.ds(core * half + k * piece, piece)]
+
+    def send_right(origin, k, own=False):
         return pltpu.make_async_remote_copy(
-            part(origin, core, k),
+            own_part(k) if own else part(origin, core, k),
             part(origin, core, k),
             right_send.at[origin, k],
             right_recv.at[origin, k],
@@ -114,9 +117,9 @@
             device_id_type=MESH,
         )
 
-    def send_left(origin, k):
+    def send_left(origin, k, own=False):
         return pltpu.make_async_remote_copy(
-            part(origin, core, k),
+            own_part(k) if own else part(origin, core, k),
             part(origin, core, k),
             left_send.at[origin, k],
             left_recv.at[origin, k],
@@ -139,11 +142,9 @@
         def _():
             action()
 
-    own_load.wait()
-    tiles[z] = raw[...].reshape(CELLS, C)
     for k in range(PIECES):
-        when(has_right, lambda: send_right(z, k).start())
-        when(has_left, lambda: send_left(z, k).start())
+        when(has_right, lambda: send_right(z, k, own=True).start())
+        when(has_left, lambda: send_left(z, k, own=True).start())
 
     at = lax.broadcasted_iota(jnp.int32, (HALO, 1), 0)
     frame = at // ((RD + 2) * W)
@@ -152,7 +153,7 @@
     wanted = owner * CELLS + (frame * RD + (row + RD) % RD) * W + at % W
 
     def absorb(origin):
-        values = tiles[origin]
+        values = tiles[origin].reshape(CELLS, C)
         normed = scaled_rms(values.astype(jnp.float32)).astype(jnp.bfloat16)
         keyvals[origin] = jnp.dot(
             normed, w_keyval[...], preferred_element_type=jnp.float32
@@ -183,6 +184,7 @@
 
     gathered[...] = jnp.zeros_like(gathered)
     keyval_load.wait()
+    own_load.wait()
     absorb(z)
 
     def absorb_step(step):
@@ -378,10 +380,9 @@
         in_specs=[anywhere] * 5,
         out_specs=vmem,
         scratch_shapes=[
-            pltpu.VMEM((tiles_here, tile_cells, C), bf16),
             pltpu.VMEM(route.shape, jnp.int32),
             pltpu.VMEM((patches, 1, CELLS), jnp.int32),
-            pltpu.VMEM((patches, CELLS, C), bf16),
+            pltpu.VMEM((patches, tiles_here, tile_cells, C), bf16),
             pltpu.VMEM((patches, CELLS, 2 * C), bf16),
             pltpu.VMEM((HALO, C), f32),
             pltpu.VMEM((HALO, 3 * C), bf16),

time: 25.8 us -> 25.9 us (level)
  no operation moved by 1% of the time
where the time goes in v3:
time: 25.9 us; the launch traced here: 25.7 us
  Pallas kernels  25.1 us (97%)
  local copies, waits for them, and re-layouts  0.66 us (3%)
    pallas_call x1, Pallas kernels, local(): pl.pallas_call(functools.partial(block_kernel, patches, spans), out_shape...  25.1 us
    unnamed x1, local copies, waits for them, and re-layouts  0.66 us

profile of v3, /device:TPU:0, one launch (start us, length us, event | category | flops | bytes accessed | tf_op | source)
XLA Modules:
  0.0 25.7 jit_solution(7624709678064330264)
XLA Ops:
  0.0 25.1 %shard_map.55 = bf16[256,192]{1,0:T(8,128)(2,1)S(1)} custom-call(bf16[64,4,384]{2,1,0:T(4,128)(2,1)} %bitcast.7, s32[1,256]{1,0:T(1,128)} %route_ref.1, bf16[384,384]{1,0:T(8,128)(2,1)} %w_query_ref.1, bf16[384,768]{1,0:T(8,128)(2,1)} %w_keyval_ref.1, bf16[27,192,384]{2,1,0:T(8,128)(2,1)} %bitcast.6), custom_call_target="tpu_custom_call" | custom-call | tf_op jit(solution)/shard_map/pallas_call | solution.py:377
  25.1 0.7 %copy.7 = bf16[2,2,64,192]{3,2,1,0:T(8,128)(2,1)} copy(bf16[2,2,64,192]{3,2,1,0:T(8,128)(2,1)S(1)} %bitcast.5) | data formatting | bytes 196608

commit v4 on v3

--- a/solution.py
+++ b/solution.py
@@ -14,6 +14,7 @@
 FD = 2
 CELLS = FD * RD * W
 HALO = FD * (RD + 2) * W
+SHARE = HALO // 2
 PIECES = 2
 KEY_BLOCK = 1024
 
@@ -56,6 +57,8 @@
     pair_recv,
     span_send,
     span_recv,
+    mixed_send,
+    mixed_recv,
 ):
     z = lax.axis_index("patch")
     x = lax.axis_index("span")
@@ -146,9 +149,10 @@
         when(has_right, lambda: send_right(z, k, own=True).start())
         when(has_left, lambda: send_left(z, k, own=True).start())
 
-    at = lax.broadcasted_iota(jnp.int32, (HALO, 1), 0)
-    frame = at // ((RD + 2) * W)
-    row = z * RD - 1 + (at // W) % (RD + 2)
+    rows_share = (RD + 2) // 2
+    at = lax.broadcasted_iota(jnp.int32, (SHARE, 1), 0)
+    frame = at // (rows_share * W)
+    row = z * RD - 1 + core * rows_share + (at // W) % rows_share
     owner = (row + RD) // RD - 1
     wanted = owner * CELLS + (frame * RD + (row + RD) % RD) * W + at % W
 
@@ -233,6 +237,7 @@
     scale = 1.0 / math.sqrt(C)
     group = min(KEY_BLOCK // CELLS, patches)
     frame_cells = HALO // FD
+    share_cells = SHARE // FD
 
     def fold(block, carry, f):
         run_max, run_total, run_acc = carry
@@ -243,7 +248,7 @@
         bias = jnp.where(allow, 0.0, -1e30)
         bias = jnp.concatenate([bias[j] for j in range(group)], axis=-1)
         scores = lax.dot_general(
-            queries[f * frame_cells : (f + 1) * frame_cells],
+            queries[f * share_cells : (f + 1) * share_cells],
             pair[:, :C],
             (((1,), (1,)), ((), ())),
             preferred_element_type=jnp.float32,
@@ -263,40 +268,52 @@
             acc = run_acc * factor + acc
         return top, sums, acc
 
-    line = lax.broadcasted_iota(jnp.int32, (frame_cells, 1), 0)
-    line_row = z * RD - 1 + line // W
-    inside = (line_row >= 0) & (line_row < patches * RD)
-    for f in range(FD):
-        span_of = slice(f * frame_cells, (f + 1) * frame_cells)
+    line = lax.broadcasted_iota(jnp.int32, (share_cells, 1), 0)
+
+    def share_at(f, side):
+        return pl.ds(pl.multiple_of(f * frame_cells + side * share_cells, share_cells), share_cells)
+
+    def send_mixed(f, side):
+        return pltpu.make_async_remote_copy(
+            mixed.at[share_at(f, side)],
+            mixed.at[share_at(f, side)],
+            mixed_send.at[f],
+            mixed_recv.at[f],
+            device_id={"chan": other},
+            device_id_type=MESH,
+        )
+
+    def attend(f):
         carry = fold(0, (None, None, None), f)
         if patches > group:
             carry = lax.fori_loop(
                 1, patches // group, functools.partial(fold, f=f), carry
             )
         _, sums, acc = carry
-        rounded = (gathered[span_of] + acc / sums).astype(jnp.bfloat16)
-        mixed[span_of] = rounded
-        v = scaled_rms(rounded.astype(jnp.float32))
+        features = gathered[f * share_cells : (f + 1) * share_cells]
+        mixed[share_at(f, core)] = (features + acc / sums).astype(jnp.bfloat16)
+        send_mixed(f, core).start()
+
+    def activate(f, side):
+        here = share_at(f, side)
+        line_row = z * RD - 1 + side * rows_share + line // W
+        inside = (line_row >= 0) & (line_row < patches * RD)
+        v = scaled_rms(mixed[here].astype(jnp.float32))
         act = jnp.where(inside, v / (1.0 + jnp.exp(-v)), 0.0)
         before = jnp.where(line % W == 0, 0.0, pltpu.roll(act, 1, 0))
-        after = jnp.where(line % W == W - 1, 0.0, pltpu.roll(act, frame_cells - 1, 0))
-        shifted3[span_of, 0:C] = before.astype(jnp.bfloat16)
-        shifted3[span_of, C : 2 * C] = act.astype(jnp.bfloat16)
-        shifted3[span_of, 2 * C : 3 * C] = after.astype(jnp.bfloat16)
-
-    def rows_of(ref, b):
-        return jnp.concatenate(
-            [ref[f * frame_cells + b * W : f * frame_cells + b * W + band] for f in range(FD)],
-            axis=0,
-        )
-
-    def conv_time(a):
+        after = jnp.where(line % W == W - 1, 0.0, pltpu.roll(act, share_cells - 1, 0))
+        shifted3[here, 0:C] = before.astype(jnp.bfloat16)
+        shifted3[here, C : 2 * C] = act.astype(jnp.bfloat16)
+        shifted3[here, 2 * C : 3 * C] = after.astype(jnp.bfloat16)
+
+    def conv_time(f, a):
         result = None
         for b in range(3):
             at_tap = 3 * (3 * a + b)
             weights = jnp.concatenate([conv[at_tap + c] for c in range(3)], axis=-1)
+            first = f * frame_cells + b * W
             term = lax.dot_general(
-                rows_of(shifted3, b),
+                shifted3[first : first + band],
                 weights,
                 (((1,), (1,)), ((), ())),
                 preferred_element_type=jnp.float32,
@@ -314,22 +331,33 @@
             device_id_type=MESH,
         )
 
-    conv_load.wait()
-    oldest = conv_time(0)
-    ahead[1] = oldest[band:].astype(jnp.bfloat16)
-    when(has_after, lambda: send_span(1).start())
-    middle = conv_time(1)
-    ahead[0] = (oldest[:band] + middle[band:]).astype(jnp.bfloat16)
-    when(has_after, lambda: send_span(0).start())
     width = out_ref.shape[-1]
     pick_from = lax.broadcasted_iota(jnp.int32, (C, width), 0)
     pick_to = lax.broadcasted_iota(jnp.int32, (C, width), 1) + core * width
     picks = jnp.where(pick_from == pick_to, 1.0, 0.0).astype(jnp.bfloat16)
-    newest = conv_time(2) + jnp.dot(
-        rows_of(mixed, 1), picks, preferred_element_type=jnp.float32
-    )
-    total[0:band] = newest[:band]
-    total[band : 2 * band] = newest[band:] + middle[:band]
+
+    def own_mixed(f):
+        first = f * frame_cells + W
+        return jnp.dot(
+            mixed[first : first + band], picks, preferred_element_type=jnp.float32
+        )
+
+    attend(1)
+    activate(1, core)
+    attend(0)
+    activate(0, core)
+    conv_load.wait()
+    send_mixed(1, other).wait_recv()
+    activate(1, other)
+    ahead[1] = conv_time(1, 0).astype(jnp.bfloat16)
+    when(has_after, lambda: send_span(1).start())
+    middle = conv_time(1, 1)
+    send_mixed(0, other).wait_recv()
+    activate(0, other)
+    ahead[0] = (conv_time(0, 0) + middle).astype(jnp.bfloat16)
+    when(has_after, lambda: send_span(0).start())
+    total[0:band] = conv_time(0, 2) + own_mixed(0)
+    total[band : 2 * band] = conv_time(0, 1) + conv_time(1, 2) + own_mixed(1)
 
     @pl.when(x == 0)
     def _():
@@ -363,6 +391,8 @@
         return carry
 
     lax.fori_loop(0, patches, finish, 0)
+    for f in range(FD):
+        send_mixed(f, core).wait_send()
 
 
 def local(latent_tiles, route, w_query, w_keyval, conv_weight):
@@ -384,7 +414,7 @@
             pltpu.VMEM((patches, 1, CELLS), jnp.int32),
             pltpu.VMEM((patches, tiles_here, tile_cells, C), bf16),
             pltpu.VMEM((patches, CELLS, 2 * C), bf16),
-            pltpu.VMEM((HALO, C), f32),
+            pltpu.VMEM((SHARE, C), f32),
             pltpu.VMEM((HALO, 3 * C), bf16),
             pltpu.VMEM((HALO, C), bf16),
             pltpu.VMEM((FD * RD * W, width), f32),
@@ -400,6 +430,8 @@
             dma((patches, PIECES)),
             dma((patches, PIECES)),
             dma((patches, PIECES)),
+            dma((FD,)),
+            dma((FD,)),
             dma((FD,)),
             dma((FD,)),
         ],

time: 25.9 us -> 24.7 us (0.954)
  Pallas kernels: 25.1 us -> 23.9 us
    pallas_call x1, Pallas kernels: 25.1 us -> 23.9 us  [local(): pl.pallas_call(functools.partial(block_kernel, patches, spans), out_shape...]
where the time goes in v4:
time: 24.7 us; the launch traced here: 24.5 us
  Pallas kernels  23.9 us (97%)
  local copies, waits for them, and re-layouts  0.66 us (3%)
    pallas_call x1, Pallas kernels, local(): pl.pallas_call(functools.partial(block_kernel, patches, spans), out_shape...  23.9 us
    unnamed x1, local copies, waits for them, and re-layouts  0.66 us

profile of v4, /device:TPU:0, one launch (start us, length us, event | category | flops | bytes accessed | tf_op | source)
XLA Modules:
  0.0 24.5 jit_solution(14837167138288057255)
XLA Ops:
  0.0 23.9 %shard_map.55 = bf16[256,192]{1,0:T(8,128)(2,1)S(1)} custom-call(bf16[64,4,384]{2,1,0:T(4,128)(2,1)} %bitcast.7, s32[1,256]{1,0:T(1,128)} %route_ref.1, bf16[384,384]{1,0:T(8,128)(2,1)} %w_query_ref.1, bf16[384,768]{1,0:T(8,128)(2,1)} %w_keyval_ref.1, bf16[27,192,384]{2,1,0:T(8,128)(2,1)} %bitcast.6), custom_call_target="tpu_custom_call" | custom-call | tf_op jit(solution)/shard_map/pallas_call | solution.py:407
  23.9 0.7 %copy.7 = bf16[2,2,64,192]{3,2,1,0:T(8,128)(2,1)} copy(bf16[2,2,64,192]{3,2,1,0:T(8,128)(2,1)S(1)} %bitcast.5) | data formatting | bytes 196608

commit v5 on v4

--- a/solution.py
+++ b/solution.py
@@ -23,7 +23,7 @@
 
 
 def scaled_rms(wide):
-    return wide / jnp.sqrt(jnp.mean(wide * wide, axis=-1, keepdims=True) + epsilon)
+    return wide * (1.0 / jnp.sqrt(jnp.mean(wide * wide, axis=-1, keepdims=True) + epsilon))
 
 
 def block_kernel(
@@ -35,6 +35,7 @@
     w_keyval_ref,
     conv_ref,
     out_ref,
+    raw,
     places_of,
     keys_ref,
     tiles,
@@ -64,12 +65,12 @@
     x = lax.axis_index("span")
     core = lax.axis_index("chan")
     other = 1 - core
-    half = tiles.shape[1] // 2
+    half = CELLS // 2
     piece = half // PIECES
     band = RD * W
 
     barrier = pltpu.get_barrier_semaphore()
-    here, tile_cells = tiles.shape[1], tiles.shape[2]
+    here, tile_cells = raw.shape[0], raw.shape[1]
 
     def greet(near, target):
         @pl.when(near)
@@ -84,7 +85,7 @@
     greet(has_after, {"span": x + 1})
     pl.semaphore_signal(barrier, inc=1, device_id={"chan": other}, device_id_type=MESH)
 
-    own_load = pltpu.make_async_copy(tiles_ref, tiles.at[z], load_sem.at[0])
+    own_load = pltpu.make_async_copy(tiles_ref, raw, load_sem.at[0])
     own_load.start()
     keyval_load = pltpu.make_async_copy(w_keyval_ref, w_keyval, load_sem.at[1])
     keyval_load.start()
@@ -102,17 +103,16 @@
         + jnp.where(has_before, 1, 0)
         + jnp.where(has_after, 1, 0)
     )
+    own_load.wait()
+    tiles[z] = raw[...].reshape(CELLS, C)
     pl.semaphore_wait(barrier, near_count)
 
     def part(origin, side, k):
-        return tiles.at[origin, pl.ds(side * half + k * piece, piece)]
-
-    def own_part(k):
-        return tiles_ref.at[pl.ds(core * half + k * piece, piece)]
-
-    def send_right(origin, k, own=False):
+        return tiles.at[origin, pl.ds(pl.multiple_of(side * half + k * piece, piece), piece)]
+
+    def send_right(origin, k):
         return pltpu.make_async_remote_copy(
-            own_part(k) if own else part(origin, core, k),
+            part(origin, core, k),
             part(origin, core, k),
             right_send.at[origin, k],
             right_recv.at[origin, k],
@@ -120,9 +120,9 @@
             device_id_type=MESH,
         )
 
-    def send_left(origin, k, own=False):
+    def send_left(origin, k):
         return pltpu.make_async_remote_copy(
-            own_part(k) if own else part(origin, core, k),
+            part(origin, core, k),
             part(origin, core, k),
             left_send.at[origin, k],
             left_recv.at[origin, k],
@@ -146,8 +146,8 @@
             action()
 
     for k in range(PIECES):
-        when(has_right, lambda: send_right(z, k, own=True).start())
-        when(has_left, lambda: send_left(z, k, own=True).start())
+        when(has_right, lambda: send_right(z, k).start())
+        when(has_left, lambda: send_left(z, k).start())
 
     rows_share = (RD + 2) // 2
     at = lax.broadcasted_iota(jnp.int32, (SHARE, 1), 0)
@@ -157,7 +157,7 @@
     wanted = owner * CELLS + (frame * RD + (row + RD) % RD) * W + at % W
 
     def absorb(origin):
-        values = tiles[origin].reshape(CELLS, C)
+        values = tiles[origin]
         normed = scaled_rms(values.astype(jnp.float32)).astype(jnp.bfloat16)
         keyvals[origin] = jnp.dot(
             normed, w_keyval[...], preferred_element_type=jnp.float32
@@ -188,7 +188,6 @@
 
     gathered[...] = jnp.zeros_like(gathered)
     keyval_load.wait()
-    own_load.wait()
     absorb(z)
 
     def absorb_step(step):
@@ -219,10 +218,12 @@
             when(z + step < patches, from_right)
 
     pass_on(1)
+    inner = has_left & has_right
 
     def gather_step(step, carry):
+        when(jnp.logical_not(inner), lambda: absorb_step(step - 1))
         pass_on(step)
-        absorb_step(step - 1)
+        when(inner, lambda: absorb_step(step - 1))
         return carry
 
     lax.fori_loop(2, patches, gather_step, 0)
@@ -291,7 +292,7 @@
             )
         _, sums, acc = carry
         features = gathered[f * share_cells : (f + 1) * share_cells]
-        mixed[share_at(f, core)] = (features + acc / sums).astype(jnp.bfloat16)
+        mixed[share_at(f, core)] = (features + acc * (1.0 / sums)).astype(jnp.bfloat16)
         send_mixed(f, core).start()
 
     def activate(f, side):
@@ -299,7 +300,7 @@
         line_row = z * RD - 1 + side * rows_share + line // W
         inside = (line_row >= 0) & (line_row < patches * RD)
         v = scaled_rms(mixed[here].astype(jnp.float32))
-        act = jnp.where(inside, v / (1.0 + jnp.exp(-v)), 0.0)
+        act = jnp.where(inside, (0.5 * v) * (1.0 + jnp.tanh(0.5 * v)), 0.0)
         before = jnp.where(line % W == 0, 0.0, pltpu.roll(act, 1, 0))
         after = jnp.where(line % W == W - 1, 0.0, pltpu.roll(act, share_cells - 1, 0))
         shifted3[here, 0:C] = before.astype(jnp.bfloat16)
@@ -410,9 +411,10 @@
         in_specs=[anywhere] * 5,
         out_specs=vmem,
         scratch_shapes=[
+            pltpu.VMEM((tiles_here, tile_cells, C), bf16),
             pltpu.VMEM(route.shape, jnp.int32),
             pltpu.VMEM((patches, 1, CELLS), jnp.int32),
-            pltpu.VMEM((patches, tiles_here, tile_cells, C), bf16),
+            pltpu.VMEM((patches, CELLS, C), bf16),
             pltpu.VMEM((patches, CELLS, 2 * C), bf16),
             pltpu.VMEM((SHARE, C), f32),
             pltpu.VMEM((HALO, 3 * C), bf16),

time: 24.7 us -> 24.4 us (0.988)
  Pallas kernels: 23.9 us -> 23.6 us
    pallas_call x1, Pallas kernels: 23.9 us -> 23.6 us  [local(): pl.pallas_call(functools.partial(block_kernel, patches, spans), out_shape...]
where the time goes in v5:
time: 24.4 us; the launch traced here: 24.2 us
  Pallas kernels  23.6 us (97%)
  local copies, waits for them, and re-layouts  0.66 us (3%)
    pallas_call x1, Pallas kernels, local(): pl.pallas_call(functools.partial(block_kernel, patches, spans), out_shape...  23.6 us
    unnamed x1, local copies, waits for them, and re-layouts  0.66 us

profile of v5, /device:TPU:0, one launch (start us, length us, event | category | flops | bytes accessed | tf_op | source)
XLA Modules:
  0.0 24.2 jit_solution(3604566052666284857)
XLA Ops:
  0.0 23.6 %shard_map.55 = bf16[256,192]{1,0:T(8,128)(2,1)S(1)} custom-call(bf16[64,4,384]{2,1,0:T(4,128)(2,1)} %bitcast.7, s32[1,256]{1,0:T(1,128)} %route_ref.1, bf16[384,384]{1,0:T(8,128)(2,1)} %w_query_ref.1, bf16[384,768]{1,0:T(8,128)(2,1)} %w_keyval_ref.1, bf16[27,192,384]{2,1,0:T(8,128)(2,1)} %bitcast.6), custom_call_target="tpu_custom_call" | custom-call | tf_op jit(solution)/shard_map/pallas_call | solution.py:408
  23.6 0.7 %copy.7 = bf16[2,2,64,192]{3,2,1,0:T(8,128)(2,1)} copy(bf16[2,2,64,192]{3,2,1,0:T(8,128)(2,1)S(1)} %bitcast.5) | data formatting | bytes 196608

commit v6 on v5

--- a/solution.py
+++ b/solution.py
@@ -15,7 +15,7 @@
 CELLS = FD * RD * W
 HALO = FD * (RD + 2) * W
 SHARE = HALO // 2
-PIECES = 2
+PIECES = 4
 KEY_BLOCK = 1024
 
 epsilon = 1e-06

time: 24.4 us -> 24.2 us (level)
  no operation moved by 1% of the time
where the time goes in v6:
time: 24.2 us; the launch traced here: 24 us
  Pallas kernels  23.4 us (97%)
  local copies, waits for them, and re-layouts  0.66 us (3%)
    pallas_call x1, Pallas kernels, local(): pl.pallas_call(functools.partial(block_kernel, patches, spans), out_shape...  23.4 us
    unnamed x1, local copies, waits for them, and re-layouts  0.66 us

profile of v6, /device:TPU:0, one launch (start us, length us, event | category | flops | bytes accessed | tf_op | source)
XLA Modules:
  0.0 24.0 jit_solution(1318668679505198620)
XLA Ops:
  0.0 23.4 %shard_map.55 = bf16[256,192]{1,0:T(8,128)(2,1)S(1)} custom-call(bf16[64,4,384]{2,1,0:T(4,128)(2,1)} %bitcast.7, s32[1,256]{1,0:T(1,128)} %route_ref.1, bf16[384,384]{1,0:T(8,128)(2,1)} %w_query_ref.1, bf16[384,768]{1,0:T(8,128)(2,1)} %w_keyval_ref.1, bf16[27,192,384]{2,1,0:T(8,128)(2,1)} %bitcast.6), custom_call_target="tpu_custom_call" | custom-call | tf_op jit(solution)/shard_map/pallas_call | solution.py:408
  23.4 0.7 %copy.7 = bf16[2,2,64,192]{3,2,1,0:T(8,128)(2,1)} copy(bf16[2,2,64,192]{3,2,1,0:T(8,128)(2,1)S(1)} %bitcast.5) | data formatting | bytes 196608

commit v7 on v5

--- a/solution.py
+++ b/solution.py
@@ -93,8 +93,14 @@
     route_load.start()
     query_load = pltpu.make_async_copy(w_query_ref, w_query, load_sem.at[2])
     query_load.start()
-    conv_load = pltpu.make_async_copy(conv_ref, conv, load_sem.at[3])
-    conv_load.start()
+    conv_loads = [
+        pltpu.make_async_copy(
+            conv_ref.at[pl.ds(9 * a, 9)], conv.at[pl.ds(9 * a, 9)], load_sem.at[5 + a]
+        )
+        for a in range(3)
+    ]
+    for load in conv_loads:
+        load.start()
 
     near_count = (
         1
@@ -240,21 +246,21 @@
     frame_cells = HALO // FD
     share_cells = SHARE // FD
 
-    def fold(block, carry, f):
+    def fold(block, carry):
         run_max, run_total, run_acc = carry
         first = block * group
         pair = keyvals[pl.ds(first, group)].reshape(group * CELLS, 2 * C)
         codes = keys_ref[pl.ds(first, group)]
-        allow = (codes // (RD * W)) % FD == f
-        bias = jnp.where(allow, 0.0, -1e30)
-        bias = jnp.concatenate([bias[j] for j in range(group)], axis=-1)
-        scores = lax.dot_general(
-            queries[f * share_cells : (f + 1) * share_cells],
-            pair[:, :C],
-            (((1,), (1,)), ((), ())),
-            preferred_element_type=jnp.float32,
-        )
-        scores = scores * scale + bias
+        code_frame = (codes // (RD * W)) % FD
+        raw_scores = lax.dot_general(
+            queries, pair[:, :C], (((1,), (1,)), ((), ())), preferred_element_type=jnp.float32
+        )
+        parts = []
+        for f in range(FD):
+            bias = jnp.where(code_frame == f, 0.0, -1e30)
+            bias = jnp.concatenate([bias[j] for j in range(group)], axis=-1)
+            parts.append(raw_scores[f * share_cells : (f + 1) * share_cells] * scale + bias)
+        scores = jnp.concatenate(parts, axis=0)
         top = jnp.max(scores, axis=-1, keepdims=True)
         if run_max is not None:
             top = jnp.maximum(top, run_max)
@@ -284,16 +290,15 @@
             device_id_type=MESH,
         )
 
-    def attend(f):
-        carry = fold(0, (None, None, None), f)
+    def attend():
+        carry = fold(0, (None, None, None))
         if patches > group:
-            carry = lax.fori_loop(
-                1, patches // group, functools.partial(fold, f=f), carry
-            )
+            carry = lax.fori_loop(1, patches // group, fold, carry)
         _, sums, acc = carry
-        features = gathered[f * share_cells : (f + 1) * share_cells]
-        mixed[share_at(f, core)] = (features + acc * (1.0 / sums)).astype(jnp.bfloat16)
-        send_mixed(f, core).start()
+        rounded = (gathered[...] + acc * (1.0 / sums)).astype(jnp.bfloat16)
+        for f in range(FD):
+            mixed[share_at(f, core)] = rounded[f * share_cells : (f + 1) * share_cells]
+            send_mixed(f, core).start()
 
     def activate(f, side):
         here = share_at(f, side)
@@ -307,17 +312,20 @@
         shifted3[here, C : 2 * C] = act.astype(jnp.bfloat16)
         shifted3[here, 2 * C : 3 * C] = after.astype(jnp.bfloat16)
 
-    def conv_time(f, a):
+    def conv_times(times):
         result = None
         for b in range(3):
-            at_tap = 3 * (3 * a + b)
-            weights = jnp.concatenate([conv[at_tap + c] for c in range(3)], axis=-1)
-            first = f * frame_cells + b * W
+            weights = jnp.concatenate(
+                [
+                    jnp.concatenate([conv[3 * (3 * a + b) + c] for c in range(3)], axis=-1)
+                    for a in times
+                ],
+                axis=0,
+            )
+            firsts = [f * frame_cells + b * W for f in range(FD)]
+            cells = jnp.concatenate([shifted3[i : i + band] for i in firsts], axis=0)
             term = lax.dot_general(
-                shifted3[first : first + band],
-                weights,
-                (((1,), (1,)), ((), ())),
-                preferred_element_type=jnp.float32,
+                weights, cells, (((1,), (1,)), ((), ())), preferred_element_type=jnp.float32
             )
             result = term if result is None else result + term
         return result
@@ -343,57 +351,62 @@
             mixed[first : first + band], picks, preferred_element_type=jnp.float32
         )
 
-    attend(1)
-    activate(1, core)
-    attend(0)
-    activate(0, core)
-    conv_load.wait()
-    send_mixed(1, other).wait_recv()
-    activate(1, other)
-    ahead[1] = conv_time(1, 0).astype(jnp.bfloat16)
+    attend()
+    for f in range(FD):
+        activate(f, core)
+    for f in range(FD):
+        send_mixed(f, other).wait_recv()
+        activate(f, other)
+    for load in conv_loads:
+        load.wait()
+    early = conv_times((0, 1))
+    ahead[1] = early[:width, band:].astype(jnp.bfloat16)
     when(has_after, lambda: send_span(1).start())
-    middle = conv_time(1, 1)
-    send_mixed(0, other).wait_recv()
-    activate(0, other)
-    ahead[0] = (conv_time(0, 0) + middle).astype(jnp.bfloat16)
+    ahead[0] = (early[:width, :band] + early[width:, band:]).astype(jnp.bfloat16)
     when(has_after, lambda: send_span(0).start())
-    total[0:band] = conv_time(0, 2) + own_mixed(0)
-    total[band : 2 * band] = conv_time(0, 1) + conv_time(1, 2) + own_mixed(1)
+    late = conv_times((2,))
+    total[0] = late[:, :band]
+    total[1] = late[:, band:] + early[width:, :band]
+
+    def finish(step, carry):
+        for k in range(PIECES):
+
+            def left_origin():
+                when(has_right, lambda: send_right(z - step, k).wait_send())
+                when(step > 0, lambda: send_pair(z - step, core, k).wait_send())
+
+            def right_origin():
+                when(has_left, lambda: send_left(z + step, k).wait_send())
+                when(step > 0, lambda: send_pair(z + step, core, k).wait_send())
+
+            when(z - step >= 0, left_origin)
+            when(z + step < patches, right_origin)
+        return carry
+
+    lax.fori_loop(0, patches, finish, 0)
+    for f in range(FD):
+        send_mixed(f, core).wait_send()
+
+    def write(t):
+        here = slice(t * band, (t + 1) * band)
+        out_ref[here] = (total[t].T + own_mixed(t)).astype(jnp.bfloat16)
 
     @pl.when(x == 0)
     def _():
-        out_ref[...] = total[...].astype(jnp.bfloat16)
+        for t in range(FD):
+            write(t)
 
     @pl.when(has_before)
     def _():
-        for t in range(FD):
+        for t in reversed(range(FD)):
             send_span(t).wait_recv()
-            here = slice(t * band, (t + 1) * band)
-            out_ref[here] = (total[here] + behind[t].astype(jnp.float32)).astype(jnp.bfloat16)
+            total[t] += behind[t].astype(jnp.float32)
+            write(t)
 
     @pl.when(has_after)
     def _():
         for t in range(FD):
             send_span(t).wait_send()
-
-    def finish(step, carry):
-        for k in range(PIECES):
-
-            def left_origin():
-                when(has_right, lambda: send_right(z - step, k).wait_send())
-                when(step > 0, lambda: send_pair(z - step, core, k).wait_send())
-
-            def right_origin():
-                when(has_left, lambda: send_left(z + step, k).wait_send())
-                when(step > 0, lambda: send_pair(z + step, core, k).wait_send())
-
-            when(z - step >= 0, left_origin)
-            when(z + step < patches, right_origin)
-        return carry
-
-    lax.fori_loop(0, patches, finish, 0)
-    for f in range(FD):
-        send_mixed(f, core).wait_send()
 
 
 def local(latent_tiles, route, w_query, w_keyval, conv_weight):
@@ -419,13 +432,13 @@
             pltpu.VMEM((SHARE, C), f32),
             pltpu.VMEM((HALO, 3 * C), bf16),
             pltpu.VMEM((HALO, C), bf16),
-            pltpu.VMEM((FD * RD * W, width), f32),
+            pltpu.VMEM((FD, width, RD * W), f32),
             pltpu.VMEM((C, C), bf16),
             pltpu.VMEM((C, 2 * C), bf16),
             pltpu.VMEM((27, width, C), bf16),
-            pltpu.VMEM((FD, RD * W, width), bf16),
-            pltpu.VMEM((FD, RD * W, width), bf16),
-            dma((5,)),
+            pltpu.VMEM((FD, width, RD * W), bf16),
+            pltpu.VMEM((FD, width, RD * W), bf16),
+            dma((8,)),
             dma((patches, PIECES)),
             dma((patches, PIECES)),
             dma((patches, PIECES)),

time: 24.4 us -> 23.8 us (0.975)
  Pallas kernels: 23.6 us -> 23 us
    pallas_call x1, Pallas kernels: 23.6 us -> 23 us  [local(): pl.pallas_call(functools.partial(block_kernel, patches, spans), out_shape...]
where the time goes in v7:
time: 23.8 us; the launch traced here: 23.7 us
  Pallas kernels  23 us (97%)
  local copies, waits for them, and re-layouts  0.66 us (3%)
    pallas_call x1, Pallas kernels, local(): pl.pallas_call(functools.partial(block_kernel, patches, spans), out_shape...  23 us
    unnamed x1, local copies, waits for them, and re-layouts  0.66 us

profile of v7, /device:TPU:0, one launch (start us, length us, event | category | flops | bytes accessed | tf_op | source)
XLA Modules:
  0.0 23.7 jit_solution(1909318926431316368)
XLA Ops:
  0.0 23.0 %shard_map.55 = bf16[256,192]{1,0:T(8,128)(2,1)S(1)} custom-call(bf16[64,4,384]{2,1,0:T(4,128)(2,1)} %bitcast.7, s32[1,256]{1,0:T(1,128)} %route_ref.1, bf16[384,384]{1,0:T(8,128)(2,1)} %w_query_ref.1, bf16[384,768]{1,0:T(8,128)(2,1)} %w_keyval_ref.1, bf16[27,192,384]{2,1,0:T(8,128)(2,1)} %bitcast.6), custom_call_target="tpu_custom_call" | custom-call | tf_op jit(solution)/shard_map/pallas_call | solution.py:421
  23.0 0.7 %copy.7 = bf16[2,2,64,192]{3,2,1,0:T(8,128)(2,1)} copy(bf16[2,2,64,192]{3,2,1,0:T(8,128)(2,1)S(1)} %bitcast.5) | data formatting | bytes 196608

commit v8 on v7

--- a/solution.py
+++ b/solution.py
@@ -162,13 +162,13 @@
     owner = (row + RD) // RD - 1
     wanted = owner * CELLS + (frame * RD + (row + RD) % RD) * W + at % W
 
-    def absorb(origin):
-        values = tiles[origin]
+    def absorb(origin, rows):
+        values = tiles[origin, rows]
         normed = scaled_rms(values.astype(jnp.float32)).astype(jnp.bfloat16)
-        keyvals[origin] = jnp.dot(
+        keyvals[origin, rows] = jnp.dot(
             normed, w_keyval[...], preferred_element_type=jnp.float32
         ).astype(jnp.bfloat16)
-        picks = jnp.where(keys_ref[origin] == wanted, 1.0, 0.0).astype(jnp.bfloat16)
+        picks = jnp.where(keys_ref[origin, :, rows] == wanted, 1.0, 0.0).astype(jnp.bfloat16)
         gathered[...] += jnp.dot(picks, values, preferred_element_type=jnp.float32)
 
     lanes = 2 * here
@@ -194,13 +194,14 @@
 
     gathered[...] = jnp.zeros_like(gathered)
     keyval_load.wait()
-    absorb(z)
+    absorb(z, pl.ds(0, CELLS))
 
     def absorb_step(step):
         def from_pair(origin):
+            absorb(origin, pl.ds(pl.multiple_of(core * half, half), half))
             for k in range(PIECES):
                 send_pair(origin, other, k).wait_recv()
-            absorb(origin)
+            absorb(origin, pl.ds(pl.multiple_of(other * half, half), half))
 
         when(z - step >= 0, lambda: from_pair(z - step))
         when(z + step < patches, lambda: from_pair(z + step))
@@ -275,7 +276,7 @@
             acc = run_acc * factor + acc
         return top, sums, acc
 
-    line = lax.broadcasted_iota(jnp.int32, (share_cells, 1), 0)
+    line = lax.broadcasted_iota(jnp.int32, (SHARE, 1), 0)
 
     def share_at(f, side):
         return pl.ds(pl.multiple_of(f * frame_cells + side * share_cells, share_cells), share_cells)
@@ -300,17 +301,17 @@
             mixed[share_at(f, core)] = rounded[f * share_cells : (f + 1) * share_cells]
             send_mixed(f, core).start()
 
-    def activate(f, side):
-        here = share_at(f, side)
-        line_row = z * RD - 1 + side * rows_share + line // W
+    def activate(side):
+        line_row = z * RD - 1 + side * rows_share + (line // W) % rows_share
         inside = (line_row >= 0) & (line_row < patches * RD)
-        v = scaled_rms(mixed[here].astype(jnp.float32))
+        held = jnp.concatenate([mixed[share_at(f, side)] for f in range(FD)], axis=0)
+        v = scaled_rms(held.astype(jnp.float32))
         act = jnp.where(inside, (0.5 * v) * (1.0 + jnp.tanh(0.5 * v)), 0.0)
         before = jnp.where(line % W == 0, 0.0, pltpu.roll(act, 1, 0))
-        after = jnp.where(line % W == W - 1, 0.0, pltpu.roll(act, share_cells - 1, 0))
-        shifted3[here, 0:C] = before.astype(jnp.bfloat16)
-        shifted3[here, C : 2 * C] = act.astype(jnp.bfloat16)
-        shifted3[here, 2 * C : 3 * C] = after.astype(jnp.bfloat16)
+        after = jnp.where(line % W == W - 1, 0.0, pltpu.roll(act, SHARE - 1, 0))
+        columns = jnp.concatenate([before, act, after], axis=-1).astype(jnp.bfloat16)
+        for f in range(FD):
+            shifted3[share_at(f, side)] = columns[f * share_cells : (f + 1) * share_cells]
 
     def conv_times(times):
         result = None
@@ -352,21 +353,21 @@
         )
 
     attend()
-    for f in range(FD):
-        activate(f, core)
+    activate(core)
     for f in range(FD):
         send_mixed(f, other).wait_recv()
-        activate(f, other)
+    activate(other)
     for load in conv_loads:
         load.wait()
-    early = conv_times((0, 1))
-    ahead[1] = early[:width, band:].astype(jnp.bfloat16)
+    oldest = conv_times((0,))
+    ahead[1] = oldest[:, band:].astype(jnp.bfloat16)
     when(has_after, lambda: send_span(1).start())
-    ahead[0] = (early[:width, :band] + early[width:, band:]).astype(jnp.bfloat16)
+    middle = conv_times((1,))
+    ahead[0] = (oldest[:, :band] + middle[:, band:]).astype(jnp.bfloat16)
     when(has_after, lambda: send_span(0).start())
     late = conv_times((2,))
     total[0] = late[:, :band]
-    total[1] = late[:, band:] + early[width:, :band]
+    total[1] = late[:, band:] + middle[:, :band]
 
     def finish(step, carry):
         for k in range(PIECES):

time: 23.8 us -> 24.4 us (1.025)
  Pallas kernels: 23 us -> 23.6 us
    pallas_call x1, Pallas kernels: 23 us -> 23.6 us  [local(): pl.pallas_call(functools.partial(block_kernel, patches, spans), out_shape...]
where the time goes in v8:
time: 24.4 us; the launch traced here: 24.2 us
  Pallas kernels  23.6 us (97%)
  local copies, waits for them, and re-layouts  0.66 us (3%)
    pallas_call x1, Pallas kernels, local(): pl.pallas_call(functools.partial(block_kernel, patches, spans), out_shape...  23.6 us
    unnamed x1, local copies, waits for them, and re-layouts  0.66 us

profile of v8, /device:TPU:0, one launch (start us, length us, event | category | flops | bytes accessed | tf_op | source)
XLA Modules:
  0.0 24.2 jit_solution(13738081604751283329)
XLA Ops:
  0.0 23.6 %shard_map.55 = bf16[256,192]{1,0:T(8,128)(2,1)S(1)} custom-call(bf16[64,4,384]{2,1,0:T(4,128)(2,1)} %bitcast.7, s32[1,256]{1,0:T(1,128)} %route_ref.1, bf16[384,384]{1,0:T(8,128)(2,1)} %w_query_ref.1, bf16[384,768]{1,0:T(8,128)(2,1)} %w_keyval_ref.1, bf16[27,192,384]{2,1,0:T(8,128)(2,1)} %bitcast.6), custom_call_target="tpu_custom_call" | custom-call | tf_op jit(solution)/shard_map/pallas_call | solution.py:422
  23.6 0.7 %copy.7 = bf16[2,2,64,192]{3,2,1,0:T(8,128)(2,1)} copy(bf16[2,2,64,192]{3,2,1,0:T(8,128)(2,1)S(1)} %bitcast.5) | data formatting | bytes 196608

commit v9 on v7

--- a/solution.py
+++ b/solution.py
@@ -23,7 +23,7 @@
 
 
 def scaled_rms(wide):
-    return wide * (1.0 / jnp.sqrt(jnp.mean(wide * wide, axis=-1, keepdims=True) + epsilon))
+    return wide * lax.rsqrt(jnp.mean(wide * wide, axis=-1, keepdims=True) + epsilon)
 
 
 def block_kernel(
@@ -359,14 +359,15 @@
         activate(f, other)
     for load in conv_loads:
         load.wait()
-    early = conv_times((0, 1))
-    ahead[1] = early[:width, band:].astype(jnp.bfloat16)
+    oldest = conv_times((0,))
+    ahead[1] = oldest[:, band:].astype(jnp.bfloat16)
     when(has_after, lambda: send_span(1).start())
-    ahead[0] = (early[:width, :band] + early[width:, band:]).astype(jnp.bfloat16)
+    middle = conv_times((1,))
+    ahead[0] = (oldest[:, :band] + middle[:, band:]).astype(jnp.bfloat16)
     when(has_after, lambda: send_span(0).start())
     late = conv_times((2,))
     total[0] = late[:, :band]
-    total[1] = late[:, band:] + early[width:, :band]
+    total[1] = late[:, band:] + middle[:, :band]
 
     def finish(step, carry):
         for k in range(PIECES):

time: 23.8 us -> 24.3 us (1.021)
  Pallas kernels: 23 us -> 23.5 us
    pallas_call x1, Pallas kernels: 23 us -> 23.5 us  [local(): pl.pallas_call(functools.partial(block_kernel, patches, spans), out_shape...]
where the time goes in v9:
time: 24.3 us; the launch traced here: 24.2 us
  Pallas kernels  23.5 us (97%)
  local copies, waits for them, and re-layouts  0.66 us (3%)
    pallas_call x1, Pallas kernels, local(): pl.pallas_call(functools.partial(block_kernel, patches, spans), out_shape...  23.5 us
    unnamed x1, local copies, waits for them, and re-layouts  0.66 us

profile of v9, /device:TPU:0, one launch (start us, length us, event | category | flops | bytes accessed | tf_op | source)
XLA Modules:
  0.0 24.2 jit_solution(7081774856092193192)
XLA Ops:
  0.0 23.5 %shard_map.55 = bf16[256,192]{1,0:T(8,128)(2,1)S(1)} custom-call(bf16[64,4,384]{2,1,0:T(4,128)(2,1)} %bitcast.7, s32[1,256]{1,0:T(1,128)} %route_ref.1, bf16[384,384]{1,0:T(8,128)(2,1)} %w_query_ref.1, bf16[384,768]{1,0:T(8,128)(2,1)} %w_keyval_ref.1, bf16[27,192,384]{2,1,0:T(8,128)(2,1)} %bitcast.6), custom_call_target="tpu_custom_call" | custom-call | tf_op jit(solution)/shard_map/pallas_call | solution.py:422
  23.5 0.7 %copy.7 = bf16[2,2,64,192]{3,2,1,0:T(8,128)(2,1)} copy(bf16[2,2,64,192]{3,2,1,0:T(8,128)(2,1)S(1)} %bitcast.5) | data formatting | bytes 196608

commit v10 on v7

--- a/solution.py
+++ b/solution.py
@@ -60,6 +60,8 @@
     span_recv,
     mixed_send,
     mixed_recv,
+    keyval_send,
+    keyval_recv,
 ):
     z = lax.axis_index("patch")
     x = lax.axis_index("span")
@@ -162,14 +164,26 @@
     owner = (row + RD) // RD - 1
     wanted = owner * CELLS + (frame * RD + (row + RD) % RD) * W + at % W
 
-    def absorb(origin):
-        values = tiles[origin]
-        normed = scaled_rms(values.astype(jnp.float32)).astype(jnp.bfloat16)
-        keyvals[origin] = jnp.dot(
+    def project(origin, rows):
+        normed = scaled_rms(tiles[origin, rows].astype(jnp.float32)).astype(jnp.bfloat16)
+        keyvals[origin, rows] = jnp.dot(
             normed, w_keyval[...], preferred_element_type=jnp.float32
         ).astype(jnp.bfloat16)
+
+    def pick(origin):
         picks = jnp.where(keys_ref[origin] == wanted, 1.0, 0.0).astype(jnp.bfloat16)
-        gathered[...] += jnp.dot(picks, values, preferred_element_type=jnp.float32)
+        gathered[...] += jnp.dot(picks, tiles[origin], preferred_element_type=jnp.float32)
+
+    def send_keyvals(origin, side):
+        rows = pl.ds(pl.multiple_of(side * half, half), half)
+        return pltpu.make_async_remote_copy(
+            keyvals.at[origin, rows],
+            keyvals.at[origin, rows],
+            keyval_send.at[origin],
+            keyval_recv.at[origin],
+            device_id={"chan": other},
+            device_id_type=MESH,
+        )
 
     lanes = 2 * here
     spread_from = lax.broadcasted_iota(jnp.int32, (lanes, 2 * CELLS), 0)
@@ -194,13 +208,16 @@
 
     gathered[...] = jnp.zeros_like(gathered)
     keyval_load.wait()
-    absorb(z)
+    project(z, pl.ds(0, CELLS))
+    pick(z)
 
     def absorb_step(step):
         def from_pair(origin):
+            project(origin, pl.ds(pl.multiple_of(core * half, half), half))
+            send_keyvals(origin, core).start()
             for k in range(PIECES):
                 send_pair(origin, other, k).wait_recv()
-            absorb(origin)
+            pick(origin)
 
         when(z - step >= 0, lambda: from_pair(z - step))
         when(z + step < patches, lambda: from_pair(z + step))
@@ -234,6 +251,16 @@
 
     lax.fori_loop(2, patches, gather_step, 0)
     absorb_step(patches - 1)
+
+    def keyvals_here(step, carry):
+        when(z - step >= 0, lambda: send_keyvals(z - step, other).wait_recv())
+        when(z + step < patches, lambda: send_keyvals(z + step, other).wait_recv())
+        return carry
+
+    def keyvals_gone(step, carry):
+        when(z - step >= 0, lambda: send_keyvals(z - step, core).wait_send())
+        when(z + step < patches, lambda: send_keyvals(z + step, core).wait_send())
+        return carry
 
     query_load.wait()
     queries = jnp.dot(
@@ -351,6 +378,7 @@
             mixed[first : first + band], picks, preferred_element_type=jnp.float32
         )
 
+    lax.fori_loop(1, patches, keyvals_here, 0)
     attend()
     for f in range(FD):
         activate(f, core)
@@ -384,6 +412,7 @@
         return carry
 
     lax.fori_loop(0, patches, finish, 0)
+    lax.fori_loop(1, patches, keyvals_gone, 0)
     for f in range(FD):
         send_mixed(f, core).wait_send()
 
@@ -449,6 +478,8 @@
             dma((FD,)),
             dma((FD,)),
             dma((FD,)),
+            dma((patches,)),
+            dma((patches,)),
         ],
         compiler_params=pltpu.CompilerParams(
             collective_id=0, has_side_effects=True, vmem_limit_bytes=56 * 1024 * 1024

time: 23.8 us -> 23.7 us (level)
  no operation moved by 1% of the time
where the time goes in v10:
time: 23.7 us; the launch traced here: 23.5 us
  Pallas kernels  22.9 us (97%)
  local copies, waits for them, and re-layouts  0.66 us (3%)
    pallas_call x1, Pallas kernels, local(): pl.pallas_call(functools.partial(block_kernel, patches, spans), out_shape...  22.9 us
    unnamed x1, local copies, waits for them, and re-layouts  0.66 us

profile of v10, /device:TPU:0, one launch (start us, length us, event | category | flops | bytes accessed | tf_op | source)
XLA Modules:
  0.0 23.5 jit_solution(11226556620154615253)
XLA Ops:
  0.0 22.9 %shard_map.55 = bf16[256,192]{1,0:T(8,128)(2,1)S(1)} custom-call(bf16[64,4,384]{2,1,0:T(4,128)(2,1)} %bitcast.7, s32[1,256]{1,0:T(1,128)} %route_ref.1, bf16[384,384]{1,0:T(8,128)(2,1)} %w_query_ref.1, bf16[384,768]{1,0:T(8,128)(2,1)} %w_keyval_ref.1, bf16[27,192,384]{2,1,0:T(8,128)(2,1)} %bitcast.6), custom_call_target="tpu_custom_call" | custom-call | tf_op jit(solution)/shard_map/pallas_call | solution.py:450
  22.9 0.7 %copy.7 = bf16[2,2,64,192]{3,2,1,0:T(8,128)(2,1)} copy(bf16[2,2,64,192]{3,2,1,0:T(8,128)(2,1)S(1)} %bitcast.5) | data formatting | bytes 196608
